TPU v7x, 32 devices: a whole 2x2x4 slice. The times are simulated.
32 devices in a mesh: section: 4 (over y, x), rows: 8 (over z, core).
Axes of the slice: x: 2, y: 2, z: 4, core: 2. Of those that a mesh axis runs over, the one named last changes fastest.
Arguments:
- latents: bfloat16 [4, 8, 4, 640], P(None, None, None, 'rows'), may hold values from -20 to 20
- w_in: bfloat16 [3, 4, 512], replicated, may hold values from -1.75 to 1.75
- w_time: bfloat16 [3, 512, 512], replicated, may hold values from -0.15625 to 0.15625
- w_first: bfloat16 [3, 3, 512, 512], P(None, None, None, 'section'), may hold values from -0.09375 to 0.09375
- w_second: bfloat16 [3, 3, 512, 512], P(None, None, None, 'section'), may hold values from -0.09375 to 0.09375
Outputs:
- decoded: bfloat16 [128, 4, 160, 512], P('rows', None, None, 'section')
All inputs are finite; a program needn't handle non-finite values.
Results may differ from a plain program's by a relative error of at most 0.0064.
Values may be sent and summed in bfloat16 or wider, within the bound.
A program may use at most 128 MiB of HBM per device.

v0:
```python
import functools

import jax
import jax.numpy as jnp
from jax import lax
from jax.experimental import pallas as pl
from jax.experimental.pallas import tpu as pltpu
from jax.sharding import PartitionSpec as P

CH = 512
LATC = 4
GROUPS = 32
HS = 4
W = 160
CLIPS = 4
LF = 8
UPS = 4


def pick(values, places):
    return jnp.stack(
        [
            lax.dynamic_index_in_dim(values, places[i], 0, keepdims=False)
            for i in range(places.shape[0])
        ]
    )


def latent_features(picked, w_in):
    total = jnp.einsum("nqp,qh->nph", picked[0], w_in[0], preferred_element_type=jnp.float32)
    for offset in range(1, 3):
        total = total + jnp.einsum(
            "nqp,qh->nph", picked[offset], w_in[offset], preferred_element_type=jnp.float32
        )
    return total.astype(jnp.bfloat16)


def time_mix(features, residual_feats, weights, own_index, tap_index):
    activated = jax.nn.silu(features.astype(jnp.float32)).astype(jnp.bfloat16)
    total = pick(residual_feats, own_index).astype(jnp.float32)
    for offset in range(3):
        product = jnp.einsum(
            "nph,hg->npg", activated, weights[offset], preferred_element_type=jnp.float32
        )
        total = total + pick(product, tap_index[offset])
    return total.astype(jnp.bfloat16)


def grid_conv(image, weight, total):
    height = image.shape[1]
    width = image.shape[2]
    padded = jnp.pad(image, ((0, 0), (1, 1), (1, 1), (0, 0)))
    for row_off in range(3):
        for col_off in range(3):
            window = padded[:, row_off : row_off + height, col_off : col_off + width]
            total = total + jnp.einsum(
                "fhwk,ko->fhwo",
                window,
                weight[row_off, col_off],
                preferred_element_type=jnp.float32,
            )
    return total


def normed(values):
    group_width = CH // GROUPS
    frames, cells, channels = values.shape
    grouped = values.reshape(frames, cells, channels // group_width, group_width)
    mean = jnp.mean(grouped, axis=(1, 3), keepdims=True)
    centered = grouped - mean
    variance = jnp.mean(centered * centered, axis=(1, 3), keepdims=True)
    scaled = centered * lax.rsqrt(variance + 1e-06)
    return jax.nn.silu(scaled).reshape(values.shape).astype(jnp.bfloat16)


def per_device_channels(latents, w_in, w_time, w_first, w_second):
    rows_count = lax.axis_size("rows")
    quarter = w_first.shape[3]
    channels = w_time.shape[2]
    section_at = lax.axis_index("section")
    clip_frames = LF * UPS
    frames_dev = CLIPS * clip_frames // rows_count
    total_cells = HS * W
    empty_sum = jnp.zeros((frames_dev, HS, W, quarter), jnp.float32)
    gathered = lax.all_gather(latents, "rows", axis=3, tiled=True)
    flat_latents = gathered.reshape(CLIPS * LF, LATC, total_cells)
    first_frame = lax.axis_index("rows") * frames_dev
    clip_at = first_frame // clip_frames
    start_frame = first_frame % clip_frames
    window_len = min(LF, (frames_dev + 1) // UPS + 2)
    window_low = jnp.minimum(jnp.maximum(start_frame - 2, 0) // UPS, LF - window_len)
    window_ids = window_low + jnp.arange(window_len, dtype=jnp.int32)
    picked = [
        pick(flat_latents, clip_at * LF + jnp.maximum(window_ids - 2 + offset, 0))
        for offset in range(3)
    ]
    features = latent_features(picked, w_in)
    frame_ids = start_frame + jnp.arange(frames_dev, dtype=jnp.int32)
    own_index = frame_ids // UPS - window_low
    tap_index = [jnp.maximum(frame_ids - 2 + offset, 0) // UPS - window_low for offset in range(3)]
    framed = time_mix(features, features, w_time, own_index, tap_index)
    first_in = normed(framed.astype(jnp.float32)).reshape(frames_dev, HS, W, channels)
    residual = lax.dynamic_slice_in_dim(framed, section_at * quarter, quarter, 2)
    inner = grid_conv(first_in, w_first, empty_sum)
    inner_cast = inner.astype(jnp.bfloat16).reshape(frames_dev, total_cells, quarter)
    second_in = normed(inner_cast.astype(jnp.float32)).reshape(frames_dev, HS, W, quarter)
    folded = grid_conv(
        lax.all_gather(second_in, "section", axis=3, tiled=True), w_second, empty_sum
    )
    output = residual.reshape(frames_dev, HS, W, quarter).astype(jnp.float32) + folded
    return output.astype(jnp.bfloat16)


def norm_conv_kernel(split, core_ref, image_ref, mine_ref, other_ref, *rest):
    residual_ref = rest[0] if len(rest) == 4 else None
    out_ref, full_ref, padded_ref = rest[-3:]
    sections, taps, half, quarter = mine_ref.shape
    cells, channels = image_ref.shape[1:]
    group_width = CH // GROUPS

    @pl.when(pl.program_id(0) == 0)
    def _():
        core = core_ref[0]

        @pl.loop(0, taps)
        def _(tap):
            for ref, at in ((mine_ref, core), (other_ref, 1 - core)):
                rows = pl.ds(pl.multiple_of(tap * channels + at * half, half), half)
                for section in range(sections):
                    lanes = slice(section * quarter, (section + 1) * quarter)
                    full_ref[rows, lanes] = ref[section, tap]

        edge = jnp.zeros((W, 3 * channels), jnp.bfloat16)
        padded_ref[:W, :] = edge
        padded_ref[W + cells :, :] = edge

    row_group = lax.div(lax.broadcasted_iota(jnp.int32, (channels, channels), 0), group_width)
    col_group = lax.div(lax.broadcasted_iota(jnp.int32, (channels, channels), 1), group_width)
    same = jnp.where(row_group == col_group, 1.0, 0.0).astype(jnp.float32)

    def group_mean(cellwise):
        per_channel = jnp.sum(cellwise, axis=0, keepdims=True)
        total = jnp.dot(
            jnp.broadcast_to(per_channel, (8, channels)),
            same,
            precision=lax.Precision.HIGHEST,
            preferred_element_type=jnp.float32,
        )
        return total[:1] * (1.0 / (cells * group_width))

    values = image_ref[0].astype(jnp.float32)
    centered = values - group_mean(values)
    scaled = centered * lax.rsqrt(group_mean(centered * centered) + 1e-06)
    active = scaled / (1.0 + jnp.exp(-scaled))
    column = lax.rem(lax.broadcasted_iota(jnp.int32, (cells, channels), 0), W)
    inside = slice(W, W + cells)
    left = jnp.where(column == 0, 0.0, pltpu.roll(active, 1, 0))
    right = jnp.where(column == W - 1, 0.0, pltpu.roll(active, cells - 1, 0))
    padded_ref[inside, :channels] = left.astype(jnp.bfloat16)
    padded_ref[inside, channels : 2 * channels] = active.astype(jnp.bfloat16)
    padded_ref[inside, 2 * channels :] = right.astype(jnp.bfloat16)

    depth = 3 * channels
    width = 2 * quarter
    for block in range(channels // width):
        lanes = slice(block * width, (block + 1) * width)
        total = None
        for row_off in range(3):
            product = jnp.dot(
                padded_ref[row_off * W : row_off * W + cells, :],
                full_ref[row_off * depth : (row_off + 1) * depth, lanes],
                preferred_element_type=jnp.float32,
            )
            total = product if total is None else total + product
        if residual_ref is not None:
            total = total + residual_ref[0, :, lanes].astype(jnp.float32)
        total = total.astype(jnp.bfloat16)
        if split:
            out_ref[0, 2 * block] = total[:, :quarter]
            out_ref[0, 2 * block + 1] = total[:, quarter:]
        else:
            out_ref[0, :, lanes] = total


def norm_conv(image, halves, core, residual=None):
    frames, cells, channels = image.shape
    mine, other = halves
    sections, taps, half, quarter = mine.shape
    split = residual is not None
    frame_spec = pl.BlockSpec((1, cells, channels), lambda i: (i, 0, 0))
    weight_spec = pl.BlockSpec(mine.shape, lambda i: (0, 0, 0, 0))
    in_specs = [pl.BlockSpec(memory_space=pltpu.SMEM), frame_spec, weight_spec, weight_spec]
    operands = [core.reshape(1), image, mine, other]
    out_shape, out_spec = (frames, cells, channels), frame_spec
    if split:
        in_specs.append(frame_spec)
        operands.append(residual)
        out_shape = (frames, sections, cells, quarter)
        out_spec = pl.BlockSpec((1, sections, cells, quarter), lambda i: (i, 0, 0, 0))
    return pl.pallas_call(
        functools.partial(norm_conv_kernel, split),
        grid=(frames,),
        in_specs=in_specs,
        out_specs=out_spec,
        out_shape=jax.ShapeDtypeStruct(out_shape, jnp.bfloat16),
        scratch_shapes=[
            pltpu.VMEM((taps * channels, sections * quarter), jnp.bfloat16),
            pltpu.VMEM((cells + 2 * W, 3 * channels), jnp.bfloat16),
        ],
        compiler_params=pltpu.CompilerParams(vmem_limit_bytes=50 * 1024 * 1024),
        cost_estimate=pl.CostEstimate(
            flops=2 * frames * cells * taps * channels * channels,
            bytes_accessed=2 * taps * channels * channels + 4 * frames * cells * channels,
            transcendentals=frames * cells * channels,
        ),
    )(*operands)


def weight_halves(weight, core):
    rows_count = lax.axis_size("rows")
    half = weight.shape[2] // 2
    mine = lax.dynamic_slice_in_dim(weight, core * half, half, 2)
    mine = mine.reshape((9,) + mine.shape[2:])
    mine = lax.all_gather(mine, "section", axis=0, tiled=False)
    other = lax.ppermute(mine, "rows", [(i, i ^ 1) for i in range(rows_count)])
    return mine, other


def unique_frames(latents, w_in, w_time, own):
    gathered = lax.all_gather(latents, "rows", axis=3, tiled=True)
    flat_latents = gathered.reshape(CLIPS * LF, LATC, HS * W)
    clip = own // LF
    at = own % LF
    count = own.shape[0]
    places = jnp.concatenate([jnp.maximum(at - 1, 0), at])
    taps = jnp.maximum(places[:, None] - 2 + jnp.arange(3, dtype=jnp.int32), 0)
    taps = taps + jnp.concatenate([clip, clip])[:, None] * LF
    picked = pick(flat_latents, taps.reshape(-1))
    picked = picked.reshape(2 * count, 3 * LATC, HS * W)
    features = jnp.einsum(
        "nqp,qh->nph", picked, w_in.reshape(3 * LATC, -1), preferred_element_type=jnp.float32
    ).astype(jnp.bfloat16)
    activated = jax.nn.silu(features.astype(jnp.float32)).astype(jnp.bfloat16)
    before, now = activated[:count], activated[count:]
    stacked = jnp.stack(
        [
            jnp.concatenate([before, before, now], axis=2),
            jnp.concatenate([before, now, now], axis=2),
            jnp.concatenate([now, now, now], axis=2),
        ]
    )
    mixed = jnp.einsum(
        "jnpk,kg->jnpg",
        stacked,
        w_time.reshape(-1, w_time.shape[2]),
        preferred_element_type=jnp.float32,
    )
    mixed = mixed + features[count:].astype(jnp.float32)
    return mixed.astype(jnp.bfloat16)


def per_device_frames(latents, w_in, w_time, w_first, w_second):
    sections = lax.axis_size("section")
    rows_count = lax.axis_size("rows")
    section_at = lax.axis_index("section")
    quarter = w_first.shape[3]
    count = CLIPS * LF // rows_count // sections
    first = (lax.axis_index("rows") * sections + section_at) * count
    own = first + jnp.arange(count, dtype=jnp.int32)
    core = lax.axis_index("rows") % 2
    first_halves = weight_halves(w_first, core)
    second_halves = weight_halves(w_second, core)
    framed = unique_frames(latents, w_in, w_time, own)
    cells, channels = framed.shape[2:]
    inner = norm_conv(framed.reshape(3 * count, cells, channels), first_halves, core)
    inner = inner.reshape(framed.shape)
    arrived = []
    for frame in range(3):
        out = norm_conv(inner[frame], second_halves, core, framed[frame])
        parts = []
        for hop in range(sections):
            part = lax.dynamic_index_in_dim(out, section_at ^ hop, 1, keepdims=False)
            if hop > 0:
                part = lax.ppermute(part, "section", [(i, i ^ hop) for i in range(sections)])
            parts.append(part)
        arrived.append(parts)
    placed = []
    for sender in range(sections):
        frames = [
            lax.select_n(section_at, *[arrived[f][sender ^ s] for s in range(sections)])
            for f in range(3)
        ]
        placed.append(jnp.stack(frames + [frames[2]], axis=1))
    result = jnp.concatenate(placed, axis=0)
    return result.reshape((sections * count * UPS, HS, W, quarter))


def per_device(latents, w_in, w_time, w_first, w_second):
    sections = lax.axis_size("section")
    rows_count = lax.axis_size("rows")
    even = (CLIPS * LF) % (rows_count * sections) == 0
    if even and rows_count % 2 == 0 and sections > 1 and sections & (sections - 1) == 0:
        return per_device_frames(latents, w_in, w_time, w_first, w_second)
    return per_device_channels(latents, w_in, w_time, w_first, w_second)


def solution(mesh):
    in_specs = (
        P(None, None, None, "rows"),
        P(),
        P(),
        P(None, None, None, "section"),
        P(None, None, None, "section"),
    )
    out_specs = P("rows", None, None, "section")
    return jax.shard_map(
        per_device, mesh=mesh, in_specs=in_specs, out_specs=out_specs, check_vma=False
    )
```

profile of v0, /device:TPU:0, one launch (start us, length us, event | category | flops | bytes accessed | tf_op | source)
XLA Modules:
  0.0 165.9 jit_solution(13552714599739241302)
XLA Ops:
  6.5 0.0 copy-start
  6.5 0.0 copy-start.1
  6.5 0.0 all-gather.3.cloned.1.call-start
  6.5 2.0 %constant_dynamic-slice_fusion.1 = bf16[3,3,256,128]{3,2,1,0:T(8,128)(2,1)} fusion(bf16[3,3,512,128]{3,2,1,0:T(8,128)(2,1)} %param.8, s32[]{:T(128)S(6)} %select_n.267), kind=kLoop, calls=%fused_computation.72 | loop fusion | bytes 1179652 | tf_op jit(solution)/shard_map/dynamic_slice | solution.py:222
  8.6 0.0 all-gather.3.cloned.1.call-update
  8.6 0.0 all-gather.5.cloned.1.call-start
  8.7 1.9 %constant_dynamic-slice_fusion = bf16[3,3,256,128]{3,2,1,0:T(8,128)(2,1)} fusion(bf16[3,3,512,128]{3,2,1,0:T(8,128)(2,1)} %param.9, s32[]{:T(128)S(6)} %select_n.267), kind=kLoop, calls=%fused_computation.71 | loop fusion | bytes 1179652 | tf_op jit(solution)/shard_map/dynamic_slice | solution.py:222
  10.6 0.0 all-gather.5.cloned.1.call-update
  10.7 0.1 add_add_fusion
  10.7 0.1 maximum_add_fusion
  10.8 0.1 add.121
  10.9 0.7 fusion.41
  19.1 0.0 copy-done.1
  19.1 0.3 copy.13
  19.4 0.0 copy-start.2
  19.4 29.1 %all_gather.9 = bf16[4,8,4,640]{1,2,0,3:T(4,128)(2,1)} all-gather(bf16[4,8,4,80]{1,2,0,3:T(4,128)(2,1)S(1)} %copy.13), channel_id=1, replica_groups=mesh['section'=4,'rows'=8] {'rows'}, dimensions={3}, use_global_device_ids=true | all-gather | bytes 184320 | tf_op jit(solution)/shard_map/all_gather | solution.py:230
  48.5 3.1 %copy.14 = bf16[4,8,4,640]{3,1,0,2:T(8,128)(2,1)S(1)} copy(bf16[4,8,4,640]{1,2,0,3:T(4,128)(2,1)} %all_gather.9) | data formatting | bytes 327680 | tf_op jit(solution)/shard_map/all_gather | solution.py:230
  55.3 0.1 constant_dynamic-slice_fusion.2
  55.4 0.1 stack.73
  55.6 0.0 copy-done.2
  55.6 0.0 all-gather.3.cloned.1.call-done.mine_ref
  55.6 0.4 collective-permute-start
  56.1 2.3 %fusion.8 = (bf16[2,640,512]{1,2,0:T(8,128)(2,1)}, bf16[2,640,512]{1,2,0:T(8,128)(2,1)}) fusion(bf16[2,12,640]{2,1,0:T(8,128)(2,1)S(1)} %reshape.92, bf16[12,512,1]{1,0,2:T(8,128)(2,1)S(1)} %reshape.98), kind=kOutput, calls=%fused_computation.15 | convolution fusion | flops 20316160 | bytes 2664448 | tf_op jit(solution)/shard_map/nqp,qh->nph/dot_general | solution.py:240
  58.4 1.2 fusion.12
  59.6 1.5 copy.17
  61.1 1.4 fusion.40
  62.5 6.1 %fusion.9 = (bf16[1,1,640,1536]{2,3,1,0:T(8,128)(2,1)S(1)}, bf16[1,1,640,1536]{2,3,1,0:T(8,128)(2,1)}, bf16[1,1,640,1536]{2,3,1,0:T(8,128)(2,1)}) fusion(bf16[1,640,512]{1,2,0:T(8,128)(2,1)S(1)} %get-tuple-element.14, bf16[1,640,512]{1,2,0:T(8,128)(2,1)S(1)} %get-tuple-element.13), kind=kLoop, calls=%fused_computation.20 | loop fusion | flops 13762560 | bytes 7208960 | tf_op jit(solution)/shard_map/stack | solution.py:245
  68.6 20.2 %all-gather.5.cloned.1.call-done.mine_ref = bf16[4,9,256,128]{3,2,1,0:T(8,128)(2,1)} async-done(((bf16[1,9,256,128]{3,2,1,0:T(8,128)(2,1)}), bf16[4,9,256,128]{3,2,1,0:T(8,128)(2,1)}) %all-gather.5.cloned.1.call-update) | async-done | bytes 2359312 | tf_op jit(solution)/shard_map/all_gather | solution.py:224
  88.8 0.0 collective-permute-start.1
  88.8 0.0 copy-done
  88.8 5.8 %add_convert_fusion.image_ref = bf16[3,640,512]{2,1,0:T(8,128)(2,1)S(1)} fusion(bf16[1536,512,1]{1,0,2:T(8,128)(2,1)S(1)} %bitcast.139, bf16[1,1,640,1536]{2,3,1,0:T(8,128)(2,1)} %get-tuple-element.36, bf16[1,1,640,1536]{2,3,1,0:T(8,128)(2,1)} %get-tuple-element.12, bf16[1,1,640,1536]{2,3,1,0:T(8,128)(2,1)S(1)} %get-tuple-element.11, f32[640,512]{1,0:T(8,128)} %copy.17), kind=kOutput, calls=%fused_computation.6 | convolution fusion | flops 3027763200 | bytes 10747904 | tf_op jit(solution)/shard_map/jnpk,kg->jnpg/dot_general | solution.py:252
  94.6 0.1 fusion.38
  94.7 0.0 collective-permute-done.other_ref
  94.7 18.3 %shard_map.55 = bf16[3,640,512]{2,1,0:T(8,128)(2,1)S(1)} custom-call(s32[1]{0:T(128)} %bitcast.core_ref, bf16[3,640,512]{2,1,0:T(8,128)(2,1)S(1)} %add_convert_fusion.image_ref, bf16[4,9,256,128]{3,2,1,0:T(8,128)(2,1)} %all-gather.3.cloned.1.call-done.mine_ref, bf16[4,9,256,128]{3,2,1,0:T(8,128)(2,1)} %collective-permute-done.other_ref), custom_call_target="tpu_custom_call" | custom-call | flops 9059696640 | bytes 8650752 | tf_op jit(solution)/shard_map/pallas_call | solution.py:200
  113.0 0.1 fusion.39
  113.2 0.0 collective-permute-done.1.other_ref
  113.2 0.0 copy-start.3
  113.2 1.4 copy-done.3
  114.6 7.7 %shard_map.56 = bf16[1,4,640,128]{3,2,1,0:T(8,128)(2,1)S(1)} custom-call(s32[1]{0:T(128)} %bitcast.core_ref, bf16[1,640,512]{2,1,0:T(8,128)(2,1)S(1)} %get-tuple-element.8.image_ref, bf16[4,9,256,128]{3,2,1,0:T(8,128)(2,1)} %all-gather.5.cloned.1.call-done.mine_ref, bf16[4,9,256,128]{3,2,1,0:T(8,128)(2,1)} %copy-done.3, ...), custom_call_target="tpu_custom_call" | custom-call | flops 3019898880 | bytes 6029312 | tf_op jit(solution)/shard_map/pallas_call | solution.py:200
  122.3 1.5 collective-permute-start.2
  123.8 0.6 collective-permute-start.3
  124.4 1.5 collective-permute-start.4
  125.9 7.5 %shard_map.57 = bf16[1,4,640,128]{3,2,1,0:T(8,128)(2,1)S(1)} custom-call(s32[1]{0:T(128)} %bitcast.core_ref, bf16[1,640,512]{2,1,0:T(8,128)(2,1)S(1)} %get-tuple-element.10.image_ref, bf16[4,9,256,128]{3,2,1,0:T(8,128)(2,1)} %all-gather.5.cloned.1.call-done.mine_ref, bf16[4,9,256,128]{3,2,1,0:T(8,128)(2,1)} %copy-done.3, ...), custom_call_target="tpu_custom_call" | custom-call | flops 3019898880 | bytes 6029312 | tf_op jit(solution)/shard_map/pallas_call | solution.py:200
  133.4 1.5 collective-permute-start.5
  135.0 0.6 collective-permute-start.6
  135.5 7.5 %shard_map.58 = bf16[1,4,640,128]{3,2,1,0:T(8,128)(2,1)S(1)} custom-call(s32[1]{0:T(128)} %bitcast.core_ref, bf16[1,640,512]{2,1,0:T(8,128)(2,1)S(1)} %get-tuple-element.9.image_ref, bf16[4,9,256,128]{3,2,1,0:T(8,128)(2,1)} %all-gather.5.cloned.1.call-done.mine_ref, bf16[4,9,256,128]{3,2,1,0:T(8,128)(2,1)} %copy-done.3, ...), custom_call_target="tpu_custom_call" | custom-call | flops 3019898880 | bytes 6029312 | tf_op jit(solution)/shard_map/pallas_call | solution.py:200
  143.1 0.0 collective-permute-done.2
  143.1 1.5 collective-permute-start.7
  144.6 0.0 collective-permute-done.3
  144.6 1.5 collective-permute-start.10
  146.1 0.0 collective-permute-done.4
  146.1 1.5 collective-permute-start.8
  147.6 0.1 fusion.30
  147.6 0.0 collective-permute-done.5
  147.7 0.6 collective-permute-start.9
  148.3 0.0 collective-permute-done.6
  148.3 3.0 %collective-permute-done.7 = bf16[1,640,128]{2,1,0:T(8,128)(2,1)S(1)} collective-permute-done((bf16[1,640,128]{2,1,0:T(8,128)(2,1)S(1)}, bf16[1,640,128]{2,1,0:T(8,128)(2,1)S(1)}, u32[]{:S(2)}, u32[]{:S(2)}) %collective-permute-start.7) | collective-permute-done | bytes 163872 | tf_op jit(solution)/shard_map/ppermute | solution.py:284
  151.2 0.1 fusion.22
  151.3 3.3 %collective-permute-done.10 = bf16[1,640,128]{2,1,0:T(8,128)(2,1)S(1)} collective-permute-done((bf16[1,640,128]{2,1,0:T(8,128)(2,1)S(1)}, bf16[1,640,128]{2,1,0:T(8,128)(2,1)S(1)}, u32[]{:S(2)}, u32[]{:S(2)}) %collective-permute-start.10) | collective-permute-done | bytes 163872 | tf_op jit(solution)/shard_map/ppermute | solution.py:284
  154.6 1.7 %collective-permute-done.8 = bf16[1,640,128]{2,1,0:T(8,128)(2,1)S(1)} collective-permute-done((bf16[1,640,128]{2,1,0:T(8,128)(2,1)S(1)}, bf16[1,640,128]{2,1,0:T(8,128)(2,1)S(1)}, u32[]{:S(2)}, u32[]{:S(2)}) %collective-permute-start.8) | collective-permute-done | bytes 163872 | tf_op jit(solution)/shard_map/ppermute | solution.py:284
  156.3 0.0 collective-permute-done.9
  156.3 0.1 fusion.14
  156.4 2.7 %maximum_maximum_fusion = bf16[4,4,640,128]{3,2,1,0:T(8,128)(2,1)} fusion(bf16[1,1,640,128]{3,2,1,0:T(8,128)(2,1)S(1)} %get-tuple-element.24, bf16[1,1,640,128]{3,2,1,0:T(8,128)(2,1)S(1)} %get-tuple-element.20, bf16[1,1,640,128]{3,2,1,0:T(8,128)(2,1)S(1)} %get-tuple-element.16, bf16[1,1,640,128]{3,2,1,0:T(8,128)(2,1)S(1)} %get-tuple-element.25, ...), kind=kLoop, calls=%fused_computation.16 | loop fusion | flops 19660800 | bytes 4587520 | tf_op jit(solution)/shard_map/concatenate | solution.py:294
  (6 shorter events, 0.2 us)
Async XLA Ops:
  6.5 82.2 %copy-start = (bf16[3,512,512]{2,1,0:T(8,128)(2,1)S(1)}, bf16[3,512,512]{2,1,0:T(8,128)(2,1)}, u32[]{:S(2)}) copy-start(bf16[3,512,512]{2,1,0:T(8,128)(2,1)} %param.7) | copy-start | bytes 4718596
  6.5 12.5 %copy-start.1 = (bf16[4,8,4,80]{3,2,1,0:T(4,128)(2,1)S(1)}, bf16[4,8,4,80]{3,2,1,0:T(4,128)(2,1)}, u32[]{:S(2)}) copy-start(bf16[4,8,4,80]{3,2,1,0:T(4,128)(2,1)} %param.5) | copy-start | bytes 61444
  6.5 49.1 %all-gather.3.cloned.1.call-start = ((), (), s32[]{:S(2)}) async-start(), calls=%async_computation | async-start | bytes 2949120 | tf_op jit(solution)/shard_map/all_gather | solution.py:224
  8.6 80.1 %all-gather.5.cloned.1.call-start = ((), (), s32[]{:S(2)}) async-start(), calls=%async_computation.1 | async-start | bytes 2949120 | tf_op jit(solution)/shard_map/all_gather | solution.py:224
  19.4 36.2 %copy-start.2 = (bf16[3,4,512]{2,1,0:T(4,128)(2,1)S(1)}, bf16[3,4,512]{2,1,0:T(4,128)(2,1)}, u32[]{:S(2)}) copy-start(bf16[3,4,512]{2,1,0:T(4,128)(2,1)} %param.6) | copy-start | bytes 36868
  55.6 39.1 %collective-permute-start = (bf16[4,9,256,128]{3,2,1,0:T(8,128)(2,1)}, bf16[4,9,256,128]{3,2,1,0:T(8,128)(2,1)}, u32[]{:S(2)}, u32[]{:S(2)}) collective-permute-start(bf16[4,9,256,128]{3,2,1,0:T(8,128)(2,1)} %all-gather.3.cloned.1.call-done.mine_ref), channel_id=1, source_target_pairs={{0,1},{1,0},{2,3},{3,2},{4,5},{5,4},{6,7},{7,6},{8,9},{9,8},{10,11... | collective-permute-start | bytes 7077896 | tf_op jit(solution)/shard_map/ppermute | solution.py:225
  88.8 24.4 %collective-permute-start.1 = (bf16[4,9,256,128]{3,2,1,0:T(8,128)(2,1)}, bf16[4,9,256,128]{3,2,1,0:T(8,128)(2,1)S(1)}, u32[]{:S(2)}, u32[]{:S(2)}) collective-permute-start(bf16[4,9,256,128]{3,2,1,0:T(8,128)(2,1)} %all-gather.5.cloned.1.call-done.mine_ref), channel_id=1, source_target_pairs={{0,1},{1,0},{2,3},{3,2},{4,5},{5,4},{6,7},{7,6},{8,9},{9,8},{10,11... | collective-permute-start | bytes 7077896 | tf_op jit(solution)/shard_map/ppermute | solution.py:225
  113.2 1.4 copy-start.3
  122.3 20.8 %collective-permute-start.2 = (bf16[1,640,128]{2,1,0:T(8,128)(2,1)S(1)}, bf16[1,640,128]{2,1,0:T(8,128)(2,1)S(1)}, u32[]{:S(2)}, u32[]{:S(2)}) collective-permute-start(bf16[1,640,128]{2,1,0:T(8,128)(2,1)S(1)} %get-tuple-element.29), channel_id=1, source_target_pairs={{0,8},{8,0},{16,24},{24,16},{1,9},{9,1},{17,25},{25,17},{2,10},{10... | collective-permute-start | bytes 491528 | tf_op jit(solution)/shard_map/ppermute | solution.py:284
  123.8 20.8 %collective-permute-start.3 = (bf16[1,640,128]{2,1,0:T(8,128)(2,1)S(1)}, bf16[1,640,128]{2,1,0:T(8,128)(2,1)S(1)}, u32[]{:S(2)}, u32[]{:S(2)}) collective-permute-start(bf16[1,640,128]{2,1,0:T(8,128)(2,1)S(1)} %get-tuple-element.27), channel_id=1, source_target_pairs={{0,16},{8,24},{16,0},{24,8},{1,17},{9,25},{17,1},{25,9},{2,18},{10... | collective-permute-start | bytes 491528 | tf_op jit(solution)/shard_map/ppermute | solution.py:284
  124.4 21.7 %collective-permute-start.4 = (bf16[1,640,128]{2,1,0:T(8,128)(2,1)S(1)}, bf16[1,640,128]{2,1,0:T(8,128)(2,1)S(1)}, u32[]{:S(2)}, u32[]{:S(2)}) collective-permute-start(bf16[1,640,128]{2,1,0:T(8,128)(2,1)S(1)} %get-tuple-element.28), channel_id=1, source_target_pairs={{0,24},{8,16},{16,8},{24,0},{1,25},{9,17},{17,9},{25,1},{2,26},{10... | collective-permute-start | bytes 491528 | tf_op jit(solution)/shard_map/ppermute | solution.py:284
  133.4 14.2 %collective-permute-start.5 = (bf16[1,640,128]{2,1,0:T(8,128)(2,1)S(1)}, bf16[1,640,128]{2,1,0:T(8,128)(2,1)S(1)}, u32[]{:S(2)}, u32[]{:S(2)}) collective-permute-start(bf16[1,640,128]{2,1,0:T(8,128)(2,1)S(1)} %get-tuple-element.32), channel_id=1, source_target_pairs={{0,8},{8,0},{16,24},{24,16},{1,9},{9,1},{17,25},{25,17},{2,10},{10... | collective-permute-start | bytes 491528 | tf_op jit(solution)/shard_map/ppermute | solution.py:284
  135.0 13.3 %collective-permute-start.6 = (bf16[1,640,128]{2,1,0:T(8,128)(2,1)S(1)}, bf16[1,640,128]{2,1,0:T(8,128)(2,1)S(1)}, u32[]{:S(2)}, u32[]{:S(2)}) collective-permute-start(bf16[1,640,128]{2,1,0:T(8,128)(2,1)S(1)} %get-tuple-element.30), channel_id=1, source_target_pairs={{0,16},{8,24},{16,0},{24,8},{1,17},{9,25},{17,1},{25,9},{2,18},{10... | collective-permute-start | bytes 491528 | tf_op jit(solution)/shard_map/ppermute | solution.py:284
  143.1 8.1 %collective-permute-start.7 = (bf16[1,640,128]{2,1,0:T(8,128)(2,1)S(1)}, bf16[1,640,128]{2,1,0:T(8,128)(2,1)S(1)}, u32[]{:S(2)}, u32[]{:S(2)}) collective-permute-start(bf16[1,640,128]{2,1,0:T(8,128)(2,1)S(1)} %get-tuple-element.31), channel_id=1, source_target_pairs={{0,24},{8,16},{16,8},{24,0},{1,25},{9,17},{17,9},{25,1},{2,26},{10... | collective-permute-start | bytes 491528 | tf_op jit(solution)/shard_map/ppermute | solution.py:284
  144.6 10.0 %collective-permute-start.10 = (bf16[1,640,128]{2,1,0:T(8,128)(2,1)S(1)}, bf16[1,640,128]{2,1,0:T(8,128)(2,1)S(1)}, u32[]{:S(2)}, u32[]{:S(2)}) collective-permute-start(bf16[1,640,128]{2,1,0:T(8,128)(2,1)S(1)} %get-tuple-element.34), channel_id=1, source_target_pairs={{0,24},{8,16},{16,8},{24,0},{1,25},{9,17},{17,9},{25,1},{2,26},{10... | collective-permute-start | bytes 491528 | tf_op jit(solution)/shard_map/ppermute | solution.py:284
  146.1 10.2 %collective-permute-start.8 = (bf16[1,640,128]{2,1,0:T(8,128)(2,1)S(1)}, bf16[1,640,128]{2,1,0:T(8,128)(2,1)S(1)}, u32[]{:S(2)}, u32[]{:S(2)}) collective-permute-start(bf16[1,640,128]{2,1,0:T(8,128)(2,1)S(1)} %get-tuple-element.35), channel_id=1, source_target_pairs={{0,8},{8,0},{16,24},{24,16},{1,9},{9,1},{17,25},{25,17},{2,10},{10... | collective-permute-start | bytes 491528 | tf_op jit(solution)/shard_map/ppermute | solution.py:284
  147.7 8.7 %collective-permute-start.9 = (bf16[1,640,128]{2,1,0:T(8,128)(2,1)S(1)}, bf16[1,640,128]{2,1,0:T(8,128)(2,1)S(1)}, u32[]{:S(2)}, u32[]{:S(2)}) collective-permute-start(bf16[1,640,128]{2,1,0:T(8,128)(2,1)S(1)} %get-tuple-element.33), channel_id=1, source_target_pairs={{0,16},{8,24},{16,0},{24,8},{1,17},{9,25},{17,1},{25,9},{2,18},{10... | collective-permute-start | bytes 491528 | tf_op jit(solution)/shard_map/ppermute | solution.py:284
Sparse Core Ops, SparseCore 0:
  9.2 40.1 all-gather.2
  51.2 37.4 all-gather.4
where the time goes:
time: 166 us
  Pallas kernels  41 us (25%)
  blocking collectives  29.1 us (18%)
  waiting for transfers between devices  28.2 us (17%)
  between operations  24.9 us (15%)
  local copies, waits for them, and re-layouts  13.1 us (8%)
  starting transfers between devices  11.2 us (7%)
  other arithmetic  10.4 us (6%)
  matrix products  8.09 us (5%)
    pallas_call x4, Pallas kernels, norm_conv(): pl.pallas_call(functools.partial(norm_conv_kernel, split), grid=(frames,)...  41 us
    all_gather x1, blocking collectives, unique_frames(): gathered = lax.all_gather(latents, 'rows', axis=3, tiled=True)  29.1 us
    all_gather x2, waiting for transfers between devices, weight_halves(): mine = lax.all_gather(mine, 'section', axis=0, tiled=False)  20.2 us
    ppermute x9, starting transfers between devices, per_device_frames(): lax.ppermute(part, 'section', [(i, i ^ hop) for i in range(sections)])  10.7 us
    ppermute x9, waiting for transfers between devices, per_device_frames(): lax.ppermute(part, 'section', [(i, i ^ hop) for i in range(sections)])  7.97 us
    another operation x1, other arithmetic, unique_frames(): jnp.stack([jnp.concatenate([before, before, now], axis=2), jnp.concatenat...  6.14 us
    dot_general x1, matrix products, unique_frames(): jnp.einsum('jnpk,kg->jnpg', stacked, w_time.reshape(-1, w_time.shape[2]),...  5.79 us
    dynamic_slice x2, local copies, waits for them, and re-layouts, weight_halves(): mine = lax.dynamic_slice_in_dim(weight, core * half, half, 2)  3.99 us
  transfers between devices with their start and end apart: 13, of which 4 were waited for; matrix products, arithmetic and copies ran while one was open for 15% of the time, Pallas kernels for 20%

commit v1 on v0

--- a/solution.py
+++ b/solution.py
@@ -216,14 +216,15 @@
     )(*operands)
 
 
-def weight_halves(weight, core):
-    rows_count = lax.axis_size("rows")
+def gather_half(weight, core):
     half = weight.shape[2] // 2
     mine = lax.dynamic_slice_in_dim(weight, core * half, half, 2)
-    mine = mine.reshape((9,) + mine.shape[2:])
-    mine = lax.all_gather(mine, "section", axis=0, tiled=False)
-    other = lax.ppermute(mine, "rows", [(i, i ^ 1) for i in range(rows_count)])
-    return mine, other
+    return lax.all_gather(mine.reshape((9,) + mine.shape[2:]), "section", axis=0, tiled=False)
+
+
+def swap_half(mine):
+    rows_count = lax.axis_size("rows")
+    return mine, lax.ppermute(mine, "rows", [(i, i ^ 1) for i in range(rows_count)])
 
 
 def unique_frames(latents, w_in, w_time, own):
@@ -268,12 +269,15 @@
     first = (lax.axis_index("rows") * sections + section_at) * count
     own = first + jnp.arange(count, dtype=jnp.int32)
     core = lax.axis_index("rows") % 2
-    first_halves = weight_halves(w_first, core)
-    second_halves = weight_halves(w_second, core)
+    first_halves = swap_half(gather_half(w_first, core))
+    second_mine = gather_half(w_second, core)
     framed = unique_frames(latents, w_in, w_time, own)
     cells, channels = framed.shape[2:]
-    inner = norm_conv(framed.reshape(3 * count, cells, channels), first_halves, core)
-    inner = inner.reshape(framed.shape)
+    early = norm_conv(framed[:2].reshape(2 * count, cells, channels), first_halves, core)
+    reached = early[0, 0, 0].astype(jnp.float32) < 1e30
+    second_halves = swap_half(jnp.where(reached, second_mine, jnp.zeros_like(second_mine)))
+    early = early.reshape(framed[:2].shape)
+    inner = [early[0], early[1], norm_conv(framed[2], first_halves, core)]
     arrived = []
     for frame in range(3):
         out = norm_conv(inner[frame], second_halves, core, framed[frame])

time: 166 us -> 153 us (0.922)
  waiting for transfers between devices: 28.2 us -> 11.6 us
  matrix products: 8.09 us -> 5.39 us
  local copies, waits for them, and re-layouts: 13.1 us -> 15.6 us
  Pallas kernels: 41 us -> 43 us
    all_gather x2, waiting for transfers between devices: 20.2 us -> 3.62 us  [gather_half(): lax.all_gather(mine.reshape((9,) + mine.shape[2:]), 'section', axis=0, ti...]
    select_n x0 -> x1, other arithmetic: none -> 3.23 us  [per_device_frames(): jnp.where(reached, second_mine, jnp.zeros_like(second_mine))]
    dot_general x1, matrix products: 5.79 us -> 3.44 us  [unique_frames(): jnp.einsum('jnpk,kg->jnpg', stacked, w_time.reshape(-1, w_time.shape[2]),...]
    pallas_call x4 -> x5, Pallas kernels: 41 us -> 43 us  [norm_conv(): pl.pallas_call(functools.partial(norm_conv_kernel, split), grid=(frames,)...]
  transfers between devices with their start and end apart: 13 -> 13, of which waited for: 4 -> 4; matrix products, arithmetic and copies ran while one was open for 15% -> 15% of each run, Pallas kernels for 20% -> 23%
where the time goes in v1:
time: 153 us
  Pallas kernels  43 us (28%)
  blocking collectives  29.1 us (19%)
  between operations  25.5 us (17%)
  local copies, waits for them, and re-layouts  15.6 us (10%)
  waiting for transfers between devices  11.6 us (8%)
  other arithmetic  11.3 us (7%)
  starting transfers between devices  11.2 us (7%)
  matrix products  5.39 us (4%)
    pallas_call x5, Pallas kernels, norm_conv(): pl.pallas_call(functools.partial(norm_conv_kernel, split), grid=(frames,)...  43 us
    all_gather x1, blocking collectives, unique_frames(): gathered = lax.all_gather(latents, 'rows', axis=3, tiled=True)  29.1 us
    ppermute x9, starting transfers between devices, per_device_frames(): lax.ppermute(part, 'section', [(i, i ^ hop) for i in range(sections)])  10.7 us
    ppermute x9, waiting for transfers between devices, per_device_frames(): lax.ppermute(part, 'section', [(i, i ^ hop) for i in range(sections)])  7.92 us
    another operation x1, other arithmetic, unique_frames(): jnp.stack([jnp.concatenate([before, before, now], axis=2), jnp.concatenat...  4.88 us
    dynamic_slice x2, local copies, waits for them, and re-layouts, gather_half(): mine = lax.dynamic_slice_in_dim(weight, core * half, half, 2)  4 us
    all_gather x2, waiting for transfers between devices, gather_half(): lax.all_gather(mine.reshape((9,) + mine.shape[2:]), 'section', axis=0, ti...  3.62 us
    dot_general x1, matrix products, unique_frames(): jnp.einsum('jnpk,kg->jnpg', stacked, w_time.reshape(-1, w_time.shape[2]),...  3.44 us
  transfers between devices with their start and end apart: 13, of which 4 were waited for; matrix products, arithmetic and copies ran while one was open for 15% of the time, Pallas kernels for 23%

profile of v1, /device:TPU:0, one launch (start us, length us, event | category | flops | bytes accessed | tf_op | source)
XLA Modules:
  0.0 152.6 jit_solution(8277866117439746019)
XLA Ops:
  6.5 2.0 %constant_dynamic-slice_fusion.1 = bf16[3,3,256,128]{3,2,1,0:T(8,128)(2,1)} fusion(bf16[3,3,512,128]{3,2,1,0:T(8,128)(2,1)} %param.8, s32[]{:T(128)S(6)} %select_n.275), kind=kLoop, calls=%fused_computation.73 | loop fusion | bytes 1179652 | tf_op jit(solution)/shard_map/dynamic_slice | solution.py:221
  8.6 0.0 all-gather.3.cloned.1.call-update
  8.6 0.0 all-gather.5.cloned.1.call-start
  8.7 2.0 %constant_dynamic-slice_fusion = bf16[3,3,256,128]{3,2,1,0:T(8,128)(2,1)} fusion(bf16[3,3,512,128]{3,2,1,0:T(8,128)(2,1)} %param.9, s32[]{:T(128)S(6)} %select_n.275), kind=kLoop, calls=%fused_computation.72 | loop fusion | bytes 1179652 | tf_op jit(solution)/shard_map/dynamic_slice | solution.py:221
  10.6 0.0 all-gather.5.cloned.1.call-update
  10.7 0.1 add_add_fusion
  10.7 0.1 maximum_add_fusion
  10.8 0.1 add.121
  10.9 0.7 fusion.41
  19.0 0.3 copy.13
  19.3 0.0 copy-start.5
  19.3 29.1 %all_gather.9 = bf16[4,8,4,640]{1,2,0,3:T(4,128)(2,1)} all-gather(bf16[4,8,4,80]{1,2,0,3:T(4,128)(2,1)S(1)} %copy.13), channel_id=1, replica_groups=mesh['section'=4,'rows'=8] {'rows'}, dimensions={3}, use_global_device_ids=true | all-gather | bytes 184320 | tf_op jit(solution)/shard_map/all_gather | solution.py:231
  48.4 3.1 %copy.14 = bf16[4,8,4,640]{3,1,0,2:T(8,128)(2,1)S(1)} copy(bf16[4,8,4,640]{1,2,0,3:T(4,128)(2,1)} %all_gather.9) | data formatting | bytes 327680 | tf_op jit(solution)/shard_map/all_gather | solution.py:231
  55.2 0.0 all-gather.3.cloned.1.call-done.mine_ref
  55.3 0.4 collective-permute-start
  55.7 0.1 constant_dynamic-slice_fusion.2
  55.8 0.1 stack.73
  55.9 0.0 copy-done.5
  55.9 2.0 %fusion.8 = (bf16[2,640,512]{1,2,0:T(8,128)(2,1)}, bf16[2,640,512]{1,2,0:T(8,128)(2,1)S(1)}) fusion(bf16[2,12,640]{2,1,0:T(8,128)(2,1)S(1)} %reshape.95, bf16[12,512,1]{1,0,2:T(8,128)(2,1)S(1)} %reshape.101), kind=kOutput, calls=%fused_computation.15 | convolution fusion | flops 20316160 | bytes 2664448 | tf_op jit(solution)/shard_map/nqp,qh->nph/dot_general | solution.py:241
  57.9 0.1 fusion.12
  58.0 1.6 %copy.17 = f32[640,512]{1,0:T(8,128)} copy(f32[640,512]{0,1:T(8,128)S(1)} %fusion.12) | data formatting | bytes 2621440 | tf_op jit(solution)/shard_map/add | solution.py:259
  59.6 1.4 fusion.40
  61.0 0.0 copy-start.3
  61.0 4.9 %fusion.9 = (bf16[1,1,640,1536]{2,3,1,0:T(8,128)(2,1)S(1)}, bf16[1,1,640,1536]{2,3,1,0:T(8,128)(2,1)S(1)}, bf16[1,1,640,1536]{2,3,1,0:T(8,128)(2,1)S(1)}) fusion(bf16[1,640,512]{1,2,0:T(8,128)(2,1)S(1)} %get-tuple-element.13, bf16[1,640,512]{1,2,0:T(8,128)(2,1)S(1)} %get-tuple-element.12), kind=kLoop, calls=%fused_computation.21 | loop fusion | flops 13762560 | bytes 7208960 | tf_op jit(solution)/shard_map/stack | solution.py:246
  65.9 0.0 copy-done
  65.9 3.4 %add_convert_fusion = bf16[3,640,512]{2,1,0:T(8,128)(2,1)S(1)} fusion(bf16[1536,512,1]{1,0,2:T(8,128)(2,1)S(1)} %bitcast.140, bf16[1,1,640,1536]{2,3,1,0:T(8,128)(2,1)S(1)} %get-tuple-element.35, bf16[1,1,640,1536]{2,3,1,0:T(8,128)(2,1)S(1)} %get-tuple-element.11, bf16[1,1,640,1536]{2,3,1,0:T(8,128)(2,1)S(1)} %get-tuple-element.10, f32[640,512]{1,0:T(8,128)S(1)} %copy-done.3), kind=kOutput, calls=%fused_computation.6 | convolution fusion | flops 3027763200 | bytes 10747904 | tf_op jit(solution)/shard_map/jnpk,kg->jnpg/dot_general | solution.py:253
  69.3 0.1 slice.74.image_ref
  69.4 0.0 collective-permute-done.other_ref
  69.5 1.2 copy-done.2
  70.7 13.3 %shard_map.55 = bf16[2,640,512]{2,1,0:T(8,128)(2,1)S(1)} custom-call(s32[1]{0:T(128)} %bitcast.core_ref, bf16[2,640,512]{2,1,0:T(8,128)(2,1)S(1)} %slice.74.image_ref, bf16[4,9,256,128]{3,2,1,0:T(8,128)(2,1)} %all-gather.3.cloned.1.call-done.mine_ref, bf16[4,9,256,128]{3,2,1,0:T(8,128)(2,1)} %collective-permute-done.other_ref), custom_call_target="tpu_custom_call" | custom-call | flops 6039797760 | bytes 7340032 | tf_op jit(solution)/shard_map/pallas_call | solution.py:200
  84.0 0.5 slice.76
  85.2 3.6 %all-gather.5.cloned.1.call-done = bf16[4,9,256,128]{3,2,1,0:T(8,128)(2,1)} async-done(((bf16[1,9,256,128]{3,2,1,0:T(8,128)(2,1)}), bf16[4,9,256,128]{3,2,1,0:T(8,128)(2,1)}) %all-gather.5.cloned.1.call-update) | async-done | bytes 2359312 | tf_op jit(solution)/shard_map/all_gather | solution.py:222
  88.8 3.2 %broadcast_select_fusion.mine_ref = bf16[4,9,256,128]{3,2,1,0:T(8,128)(2,1)} fusion(bf16[4,9,256,128]{3,2,1,0:T(8,128)(2,1)} %all-gather.5.cloned.1.call-done, pred[]{:T(512)} %bitcast.17), kind=kLoop, calls=%fused_computation.20 | loop fusion | flops 1179648 | bytes 4718593 | tf_op jit(solution)/shard_map/jit(_where)/select_n | solution.py:278
  92.0 0.0 collective-permute-start.1
  92.0 1.8 %fusion.38 = (bf16[1,640,512]{2,1,0:T(8,128)(2,1)S(1)}, bf16[1,640,512]{2,1,0:T(8,128)(2,1)S(1)}, bf16[1,640,512]{2,1,0:T(8,128)(2,1)S(1)}) fusion(bf16[3,640,512]{2,1,0:T(8,128)(2,1)} %copy-done.2), kind=kLoop, calls=%fused_computation.84 | loop fusion | bytes 3932160 | tf_op jit(solution)/shard_map/slice | solution.py:283
  93.8 0.1 fusion.39
  93.8 0.4 copy-done.1
  94.2 7.0 %shard_map.58.image_ref = bf16[1,640,512]{2,1,0:T(8,128)(2,1)S(1)} custom-call(s32[1]{0:T(128)} %bitcast.core_ref, bf16[1,640,512]{2,1,0:T(8,128)(2,1)S(1)} %get-tuple-element.6.image_ref.rest_0_, bf16[4,9,256,128]{3,2,1,0:T(8,128)(2,1)S(1)} %copy-done.1, bf16[4,9,256,128]{3,2,1,0:T(8,128)(2,1)} %collective-permute-done.other_ref), custom_call_target="tpu_custom_call" | custom-call | flops 3019898880 | bytes 6029312 | tf_op jit(solution)/shard_map/pallas_call | solution.py:200
  101.2 0.0 collective-permute-done.1.other_ref
  101.2 7.5 %shard_map.59 = bf16[1,4,640,128]{3,2,1,0:T(8,128)(2,1)S(1)} custom-call(s32[1]{0:T(128)} %bitcast.core_ref, bf16[1,640,512]{2,1,0:T(8,128)(2,1)S(1)} %shard_map.58.image_ref, bf16[4,9,256,128]{3,2,1,0:T(8,128)(2,1)} %broadcast_select_fusion.mine_ref, bf16[4,9,256,128]{3,2,1,0:T(8,128)(2,1)} %collective-permute-done.1.other_ref, ...), custom_call_target="tpu_custom_call" | custom-call | flops 3019898880 | bytes 6029312 | tf_op jit(solution)/shard_map/pallas_call | solution.py:200
  108.8 1.5 %collective-permute-start.8 = (bf16[1,640,128]{2,1,0:T(8,128)(2,1)S(1)}, bf16[1,640,128]{2,1,0:T(8,128)(2,1)S(1)}, u32[]{:S(2)}, u32[]{:S(2)}) collective-permute-start(bf16[1,640,128]{2,1,0:T(8,128)(2,1)S(1)} %get-tuple-element.34), channel_id=1, source_target_pairs={{0,8},{8,0},{16,24},{24,16},{1,9},{9,1},{17,25},{25,17},{2,10},{10... | collective-permute-start | bytes 491528 | tf_op jit(solution)/shard_map/ppermute | solution.py:288
  110.3 0.6 collective-permute-start.9
  110.9 1.5 collective-permute-start.10
  112.3 7.5 %shard_map.57 = bf16[1,4,640,128]{3,2,1,0:T(8,128)(2,1)S(1)} custom-call(s32[1]{0:T(128)} %bitcast.core_ref, bf16[1,640,512]{2,1,0:T(8,128)(2,1)S(1)} %get-tuple-element.9.image_ref, bf16[4,9,256,128]{3,2,1,0:T(8,128)(2,1)} %broadcast_select_fusion.mine_ref, bf16[4,9,256,128]{3,2,1,0:T(8,128)(2,1)} %collective-permute-done.1.other_ref, ...), custom_call_target="tpu_custom_call" | custom-call | flops 3019898880 | bytes 6029312 | tf_op jit(solution)/shard_map/pallas_call | solution.py:200
  119.9 1.5 %collective-permute-start.5 = (bf16[1,640,128]{2,1,0:T(8,128)(2,1)S(1)}, bf16[1,640,128]{2,1,0:T(8,128)(2,1)S(1)}, u32[]{:S(2)}, u32[]{:S(2)}) collective-permute-start(bf16[1,640,128]{2,1,0:T(8,128)(2,1)S(1)} %get-tuple-element.31), channel_id=1, source_target_pairs={{0,8},{8,0},{16,24},{24,16},{1,9},{9,1},{17,25},{25,17},{2,10},{10... | collective-permute-start | bytes 491528 | tf_op jit(solution)/shard_map/ppermute | solution.py:288
  121.4 0.6 collective-permute-start.6
  122.0 7.7 %shard_map.56 = bf16[1,4,640,128]{3,2,1,0:T(8,128)(2,1)S(1)} custom-call(s32[1]{0:T(128)} %bitcast.core_ref, bf16[1,640,512]{2,1,0:T(8,128)(2,1)S(1)} %get-tuple-element.8.image_ref, bf16[4,9,256,128]{3,2,1,0:T(8,128)(2,1)} %broadcast_select_fusion.mine_ref, bf16[4,9,256,128]{3,2,1,0:T(8,128)(2,1)} %collective-permute-done.1.other_ref, ...), custom_call_target="tpu_custom_call" | custom-call | flops 3019898880 | bytes 6029312 | tf_op jit(solution)/shard_map/pallas_call | solution.py:200
  129.8 0.0 collective-permute-done.8
  129.8 1.5 collective-permute-start.7
  131.3 0.0 collective-permute-done.9
  131.3 1.5 collective-permute-start.2
  132.8 0.0 collective-permute-done.10
  132.8 0.6 collective-permute-start.3
  133.4 0.1 fusion.14
  133.5 0.0 collective-permute-done.5
  133.5 1.5 collective-permute-start.4
  135.0 0.0 collective-permute-done.6
  135.0 3.0 %collective-permute-done.7 = bf16[1,640,128]{2,1,0:T(8,128)(2,1)S(1)} collective-permute-done((bf16[1,640,128]{2,1,0:T(8,128)(2,1)S(1)}, bf16[1,640,128]{2,1,0:T(8,128)(2,1)S(1)}, u32[]{:S(2)}, u32[]{:S(2)}) %collective-permute-start.7) | collective-permute-done | bytes 163872 | tf_op jit(solution)/shard_map/ppermute | solution.py:288
  137.9 0.1 fusion.22
  138.0 3.2 %collective-permute-done.2 = bf16[1,640,128]{2,1,0:T(8,128)(2,1)S(1)} collective-permute-done((bf16[1,640,128]{2,1,0:T(8,128)(2,1)S(1)}, bf16[1,640,128]{2,1,0:T(8,128)(2,1)S(1)}, u32[]{:S(2)}, u32[]{:S(2)}) %collective-permute-start.2) | collective-permute-done | bytes 163872 | tf_op jit(solution)/shard_map/ppermute | solution.py:288
  141.2 0.0 collective-permute-done.3
  141.2 1.7 %collective-permute-done.4 = bf16[1,640,128]{2,1,0:T(8,128)(2,1)S(1)} collective-permute-done((bf16[1,640,128]{2,1,0:T(8,128)(2,1)S(1)}, bf16[1,640,128]{2,1,0:T(8,128)(2,1)S(1)}, u32[]{:S(2)}, u32[]{:S(2)}) %collective-permute-start.4) | collective-permute-done | bytes 163872 | tf_op jit(solution)/shard_map/ppermute | solution.py:288
  143.0 0.1 fusion.30
  143.1 2.7 %maximum_maximum_fusion = bf16[4,4,640,128]{3,2,1,0:T(8,128)(2,1)} fusion(bf16[1,1,640,128]{3,2,1,0:T(8,128)(2,1)S(1)} %get-tuple-element.23, bf16[1,1,640,128]{3,2,1,0:T(8,128)(2,1)S(1)} %get-tuple-element.19, bf16[1,1,640,128]{3,2,1,0:T(8,128)(2,1)S(1)} %get-tuple-element.15, bf16[1,1,640,128]{3,2,1,0:T(8,128)(2,1)S(1)} %get-tuple-element.24, ...), kind=kLoop, calls=%fused_computation.16 | loop fusion | flops 19660800 | bytes 4587520 | tf_op jit(solution)/shard_map/concatenate | solution.py:298
  (13 shorter events, 0.2 us)
Async XLA Ops:
  6.5 59.3 %copy-start = (bf16[3,512,512]{2,1,0:T(8,128)(2,1)S(1)}, bf16[3,512,512]{2,1,0:T(8,128)(2,1)}, u32[]{:S(2)}) copy-start(bf16[3,512,512]{2,1,0:T(8,128)(2,1)} %param.7) | copy-start | bytes 4718596
  6.5 12.5 %copy-start.4 = (bf16[4,8,4,80]{3,2,1,0:T(4,128)(2,1)S(1)}, bf16[4,8,4,80]{3,2,1,0:T(4,128)(2,1)}, u32[]{:S(2)}) copy-start(bf16[4,8,4,80]{3,2,1,0:T(4,128)(2,1)} %param.5) | copy-start | bytes 61444
  6.5 48.7 %all-gather.3.cloned.1.call-start = ((), (), s32[]{:S(2)}) async-start(), calls=%async_computation | async-start | bytes 2949120 | tf_op jit(solution)/shard_map/all_gather | solution.py:222
  8.6 80.1 %all-gather.5.cloned.1.call-start = ((), (), s32[]{:S(2)}) async-start(), calls=%async_computation.1 | async-start | bytes 2949120 | tf_op jit(solution)/shard_map/all_gather | solution.py:222
  19.3 36.6 %copy-start.5 = (bf16[3,4,512]{2,1,0:T(4,128)(2,1)S(1)}, bf16[3,4,512]{2,1,0:T(4,128)(2,1)}, u32[]{:S(2)}) copy-start(bf16[3,4,512]{2,1,0:T(4,128)(2,1)} %param.6) | copy-start | bytes 36868
  55.3 14.2 %collective-permute-start = (bf16[4,9,256,128]{3,2,1,0:T(8,128)(2,1)}, bf16[4,9,256,128]{3,2,1,0:T(8,128)(2,1)}, u32[]{:S(2)}, u32[]{:S(2)}) collective-permute-start(bf16[4,9,256,128]{3,2,1,0:T(8,128)(2,1)} %all-gather.3.cloned.1.call-done.mine_ref), channel_id=1, source_target_pairs={{0,1},{1,0},{2,3},{3,2},{4,5},{5,4},{6,7},{7,6},{8,9},{9,8},{10,11... | collective-permute-start | bytes 7077896 | tf_op jit(solution)/shard_map/ppermute | solution.py:227
  61.0 4.9 %copy-start.3 = (f32[640,512]{1,0:T(8,128)S(1)}, f32[640,512]{1,0:T(8,128)}, u32[]{:S(2)}) copy-start(f32[640,512]{1,0:T(8,128)} %copy.17) | copy-start | bytes 3932164
  69.3 1.4 copy-start.2
  92.0 9.2 %collective-permute-start.1 = (bf16[4,9,256,128]{3,2,1,0:T(8,128)(2,1)}, bf16[4,9,256,128]{3,2,1,0:T(8,128)(2,1)}, u32[]{:S(2)}, u32[]{:S(2)}) collective-permute-start(bf16[4,9,256,128]{3,2,1,0:T(8,128)(2,1)} %broadcast_select_fusion.mine_ref), channel_id=1, source_target_pairs={{0,1},{1,0},{2,3},{3,2},{4,5},{5,4},{6,7},{7,6},{8,9},{9,8},{10,11... | collective-permute-start | bytes 7077896 | tf_op jit(solution)/shard_map/ppermute | solution.py:227
  92.0 2.3 %copy-start.1 = (bf16[4,9,256,128]{3,2,1,0:T(8,128)(2,1)S(1)}, bf16[4,9,256,128]{3,2,1,0:T(8,128)(2,1)}, u32[]{:S(2)}) copy-start(bf16[4,9,256,128]{3,2,1,0:T(8,128)(2,1)} %all-gather.3.cloned.1.call-done.mine_ref) | copy-start | bytes 7077892
  108.8 21.0 %collective-permute-start.8 = (bf16[1,640,128]{2,1,0:T(8,128)(2,1)S(1)}, bf16[1,640,128]{2,1,0:T(8,128)(2,1)S(1)}, u32[]{:S(2)}, u32[]{:S(2)}) collective-permute-start(bf16[1,640,128]{2,1,0:T(8,128)(2,1)S(1)} %get-tuple-element.34), channel_id=1, source_target_pairs={{0,8},{8,0},{16,24},{24,16},{1,9},{9,1},{17,25},{25,17},{2,10},{10... | collective-permute-start | bytes 491528 | tf_op jit(solution)/shard_map/ppermute | solution.py:288
  110.3 21.0 %collective-permute-start.9 = (bf16[1,640,128]{2,1,0:T(8,128)(2,1)S(1)}, bf16[1,640,128]{2,1,0:T(8,128)(2,1)S(1)}, u32[]{:S(2)}, u32[]{:S(2)}) collective-permute-start(bf16[1,640,128]{2,1,0:T(8,128)(2,1)S(1)} %get-tuple-element.32), channel_id=1, source_target_pairs={{0,16},{8,24},{16,0},{24,8},{1,17},{9,25},{17,1},{25,9},{2,18},{10... | collective-permute-start | bytes 491528 | tf_op jit(solution)/shard_map/ppermute | solution.py:288
  110.9 21.9 %collective-permute-start.10 = (bf16[1,640,128]{2,1,0:T(8,128)(2,1)S(1)}, bf16[1,640,128]{2,1,0:T(8,128)(2,1)S(1)}, u32[]{:S(2)}, u32[]{:S(2)}) collective-permute-start(bf16[1,640,128]{2,1,0:T(8,128)(2,1)S(1)} %get-tuple-element.33), channel_id=1, source_target_pairs={{0,24},{8,16},{16,8},{24,0},{1,25},{9,17},{17,9},{25,1},{2,26},{10... | collective-permute-start | bytes 491528 | tf_op jit(solution)/shard_map/ppermute | solution.py:288
  119.9 13.5 %collective-permute-start.5 = (bf16[1,640,128]{2,1,0:T(8,128)(2,1)S(1)}, bf16[1,640,128]{2,1,0:T(8,128)(2,1)S(1)}, u32[]{:S(2)}, u32[]{:S(2)}) collective-permute-start(bf16[1,640,128]{2,1,0:T(8,128)(2,1)S(1)} %get-tuple-element.31), channel_id=1, source_target_pairs={{0,8},{8,0},{16,24},{24,16},{1,9},{9,1},{17,25},{25,17},{2,10},{10... | collective-permute-start | bytes 491528 | tf_op jit(solution)/shard_map/ppermute | solution.py:288
  121.4 13.5 %collective-permute-start.6 = (bf16[1,640,128]{2,1,0:T(8,128)(2,1)S(1)}, bf16[1,640,128]{2,1,0:T(8,128)(2,1)S(1)}, u32[]{:S(2)}, u32[]{:S(2)}) collective-permute-start(bf16[1,640,128]{2,1,0:T(8,128)(2,1)S(1)} %get-tuple-element.29), channel_id=1, source_target_pairs={{0,16},{8,24},{16,0},{24,8},{1,17},{9,25},{17,1},{25,9},{2,18},{10... | collective-permute-start | bytes 491528 | tf_op jit(solution)/shard_map/ppermute | solution.py:288
  129.8 8.1 %collective-permute-start.7 = (bf16[1,640,128]{2,1,0:T(8,128)(2,1)S(1)}, bf16[1,640,128]{2,1,0:T(8,128)(2,1)S(1)}, u32[]{:S(2)}, u32[]{:S(2)}) collective-permute-start(bf16[1,640,128]{2,1,0:T(8,128)(2,1)S(1)} %get-tuple-element.30), channel_id=1, source_target_pairs={{0,24},{8,16},{16,8},{24,0},{1,25},{9,17},{17,9},{25,1},{2,26},{10... | collective-permute-start | bytes 491528 | tf_op jit(solution)/shard_map/ppermute | solution.py:288
  131.3 9.9 %collective-permute-start.2 = (bf16[1,640,128]{2,1,0:T(8,128)(2,1)S(1)}, bf16[1,640,128]{2,1,0:T(8,128)(2,1)S(1)}, u32[]{:S(2)}, u32[]{:S(2)}) collective-permute-start(bf16[1,640,128]{2,1,0:T(8,128)(2,1)S(1)} %get-tuple-element.28), channel_id=1, source_target_pairs={{0,8},{8,0},{16,24},{24,16},{1,9},{9,1},{17,25},{25,17},{2,10},{10... | collective-permute-start | bytes 491528 | tf_op jit(solution)/shard_map/ppermute | solution.py:288
  132.8 8.4 %collective-permute-start.3 = (bf16[1,640,128]{2,1,0:T(8,128)(2,1)S(1)}, bf16[1,640,128]{2,1,0:T(8,128)(2,1)S(1)}, u32[]{:S(2)}, u32[]{:S(2)}) collective-permute-start(bf16[1,640,128]{2,1,0:T(8,128)(2,1)S(1)} %get-tuple-element.26), channel_id=1, source_target_pairs={{0,16},{8,24},{16,0},{24,8},{1,17},{9,25},{17,1},{25,9},{2,18},{10... | collective-permute-start | bytes 491528 | tf_op jit(solution)/shard_map/ppermute | solution.py:288
  133.5 9.5 %collective-permute-start.4 = (bf16[1,640,128]{2,1,0:T(8,128)(2,1)S(1)}, bf16[1,640,128]{2,1,0:T(8,128)(2,1)S(1)}, u32[]{:S(2)}, u32[]{:S(2)}) collective-permute-start(bf16[1,640,128]{2,1,0:T(8,128)(2,1)S(1)} %get-tuple-element.27), channel_id=1, source_target_pairs={{0,24},{8,16},{16,8},{24,0},{1,25},{9,17},{17,9},{25,1},{2,26},{10... | collective-permute-start | bytes 491528 | tf_op jit(solution)/shard_map/ppermute | solution.py:288
Sparse Core Ops, SparseCore 0:
  9.2 40.1 all-gather.2
  51.2 37.4 all-gather.4

commit v2 on v1

--- a/solution.py
+++ b/solution.py
@@ -222,6 +222,24 @@
     return lax.all_gather(mine.reshape((9,) + mine.shape[2:]), "section", axis=0, tiled=False)
 
 
+def permute_half(weight, core):
+    sections = lax.axis_size("section")
+    section_at = lax.axis_index("section")
+    half = weight.shape[2] // 2
+    own = lax.dynamic_slice_in_dim(weight, core * half, half, 2)
+    own = own.reshape((9,) + own.shape[2:])
+    parts = [own] + [
+        lax.ppermute(own, "section", [(i, i ^ hop) for i in range(sections)])
+        for hop in range(1, sections)
+    ]
+    return jnp.stack(
+        [
+            lax.select_n(section_at, *[parts[sender ^ s] for s in range(sections)])
+            for sender in range(sections)
+        ]
+    )
+
+
 def swap_half(mine):
     rows_count = lax.axis_size("rows")
     return mine, lax.ppermute(mine, "rows", [(i, i ^ 1) for i in range(rows_count)])
@@ -270,14 +288,11 @@
     own = first + jnp.arange(count, dtype=jnp.int32)
     core = lax.axis_index("rows") % 2
     first_halves = swap_half(gather_half(w_first, core))
-    second_mine = gather_half(w_second, core)
+    second_halves = swap_half(permute_half(w_second, core))
     framed = unique_frames(latents, w_in, w_time, own)
     cells, channels = framed.shape[2:]
-    early = norm_conv(framed[:2].reshape(2 * count, cells, channels), first_halves, core)
-    reached = early[0, 0, 0].astype(jnp.float32) < 1e30
-    second_halves = swap_half(jnp.where(reached, second_mine, jnp.zeros_like(second_mine)))
-    early = early.reshape(framed[:2].shape)
-    inner = [early[0], early[1], norm_conv(framed[2], first_halves, core)]
+    inner = norm_conv(framed.reshape(3 * count, cells, channels), first_halves, core)
+    inner = inner.reshape(framed.shape)
     arrived = []
     for frame in range(3):
         out = norm_conv(inner[frame], second_halves, core, framed[frame])

time: 153 us -> 147 us (0.961)
  starting transfers between devices: 11.2 us -> 15.8 us
  other arithmetic: 11.3 us -> 8.62 us
  waiting for transfers between devices: 11.6 us -> 9.23 us
  local copies, waits for them, and re-layouts: 15.6 us -> 13.4 us
  Pallas kernels: 43 us -> 41 us
    ppermute x0 -> x3, starting transfers between devices: none -> 4.46 us  [permute_half(): lax.ppermute(own, 'section', [(i, i ^ hop) for i in range(sections)])]
    select_n x1 -> x0, other arithmetic: 3.23 us -> none  [per_device_frames(): jnp.where(reached, second_mine, jnp.zeros_like(second_mine))]
    another operation x1, other arithmetic: 4.88 us -> 2.24 us  [unique_frames(): jnp.stack([jnp.concatenate([before, before, now], axis=2), jnp.concatenat...]
    all_gather x2 -> x1, waiting for transfers between devices: 3.62 us -> 1.28 us  [gather_half(): lax.all_gather(mine.reshape((9,) + mine.shape[2:]), 'section', axis=0, ti...]
    another operation x0 -> x2, other arithmetic: none -> 2.15 us  [permute_half(): jnp.stack([lax.select_n(section_at, *[parts[sender ^ s] for s in range(se...]
    pallas_call x5 -> x4, Pallas kernels: 43 us -> 41 us  [norm_conv(): pl.pallas_call(functools.partial(norm_conv_kernel, split), grid=(frames,)...]
    dynamic_slice x0 -> x1, local copies, waits for them, and re-layouts: none -> 1.93 us  [permute_half(): own = lax.dynamic_slice_in_dim(weight, core * half, half, 2)]
    dynamic_slice x2 -> x1, local copies, waits for them, and re-layouts: 4 us -> 2.09 us  [gather_half(): mine = lax.dynamic_slice_in_dim(weight, core * half, half, 2)]
  transfers between devices with their start and end apart: 13 -> 15, of which waited for: 4 -> 4; matrix products, arithmetic and copies ran while one was open for 15% -> 14% of each run, Pallas kernels for 23% -> 23%
where the time goes in v2:
time: 147 us; the launch traced here: 146 us
  Pallas kernels  41 us (28%)
  blocking collectives  28.1 us (19%)
  between operations  25 us (17%)
  starting transfers between devices  15.8 us (11%)
  local copies, waits for them, and re-layouts  13.4 us (9%)
  waiting for transfers between devices  9.23 us (6%)
  other arithmetic  8.62 us (6%)
  matrix products  5.32 us (4%)
    pallas_call x4, Pallas kernels, norm_conv(): pl.pallas_call(functools.partial(norm_conv_kernel, split), grid=(frames,)...  41 us
    all_gather x1, blocking collectives, unique_frames(): gathered = lax.all_gather(latents, 'rows', axis=3, tiled=True)  28.1 us
    ppermute x9, starting transfers between devices, per_device_frames(): lax.ppermute(part, 'section', [(i, i ^ hop) for i in range(sections)])  10.7 us
    ppermute x9, waiting for transfers between devices, per_device_frames(): lax.ppermute(part, 'section', [(i, i ^ hop) for i in range(sections)])  7.93 us
    ppermute x3, starting transfers between devices, permute_half(): lax.ppermute(own, 'section', [(i, i ^ hop) for i in range(sections)])  4.46 us
    dot_general x1, matrix products, unique_frames(): jnp.einsum('jnpk,kg->jnpg', stacked, w_time.reshape(-1, w_time.shape[2]),...  3.44 us
    all_gather x1, local copies, waits for them, and re-layouts, unique_frames(): gathered = lax.all_gather(latents, 'rows', axis=3, tiled=True)  3.08 us
  transfers between devices with their start and end apart: 15, of which 4 were waited for; matrix products, arithmetic and copies ran while one was open for 14% of the time, Pallas kernels for 23%

profile of v2, /device:TPU:0, one launch (start us, length us, event | category | flops | bytes accessed | tf_op | source)
XLA Modules:
  0.0 146.4 jit_solution(17661770349460077325)
XLA Ops:
  6.5 0.0 all-gather.2.cloned.1.call-start
  6.5 2.1 %constant_dynamic-slice_fusion.1 = bf16[3,3,256,128]{3,2,1,0:T(8,128)(2,1)} fusion(bf16[3,3,512,128]{3,2,1,0:T(8,128)(2,1)} %param.8, s32[]{:T(128)S(6)} %select_n.333), kind=kLoop, calls=%fused_computation.77 | loop fusion | bytes 1179652 | tf_op jit(solution)/shard_map/dynamic_slice | solution.py:221
  8.6 0.0 all-gather.2.cloned.1.call-update
  8.7 1.9 %constant_dynamic-slice_fusion = bf16[3,3,256,128]{3,2,1,0:T(8,128)(2,1)} fusion(bf16[3,3,512,128]{3,2,1,0:T(8,128)(2,1)} %param.9, s32[]{:T(128)S(6)} %select_n.333), kind=kLoop, calls=%fused_computation.76 | loop fusion | bytes 1179652 | tf_op jit(solution)/shard_map/dynamic_slice | solution.py:229
  10.6 3.0 %collective-permute-start.2 = (bf16[9,256,128]{2,1,0:T(8,128)(2,1)}, bf16[9,256,128]{2,1,0:T(8,128)(2,1)}, u32[]{:S(2)}, u32[]{:S(2)}) collective-permute-start(bf16[9,256,128]{2,1,0:T(8,128)(2,1)} %bitcast.17), channel_id=1, source_target_pairs={{0,16},{8,24},{16,0},{24,8},{1,17},{9,25},{17,1},{25,9},{2,18},{10... | collective-permute-start | bytes 1769480 | tf_op jit(solution)/shard_map/ppermute | solution.py:232
  13.6 1.4 collective-permute-start.3
  15.0 0.1 collective-permute-start.1
  15.0 0.1 add_add_fusion
  15.1 0.1 maximum_add_fusion
  15.2 0.1 add.121
  15.3 0.7 fusion.41
  23.5 0.3 copy.13
  23.8 0.0 copy-start.4
  23.8 28.1 %all_gather.6 = bf16[4,8,4,640]{1,2,0,3:T(4,128)(2,1)} all-gather(bf16[4,8,4,80]{1,2,0,3:T(4,128)(2,1)S(1)} %copy.13), channel_id=1, replica_groups=mesh['section'=4,'rows'=8] {'rows'}, dimensions={3}, use_global_device_ids=true | all-gather | bytes 184320 | tf_op jit(solution)/shard_map/all_gather | solution.py:249
  51.9 3.1 %copy.14 = bf16[4,8,4,640]{3,1,0,2:T(8,128)(2,1)S(1)} copy(bf16[4,8,4,640]{1,2,0,3:T(4,128)(2,1)} %all_gather.6) | data formatting | bytes 327680 | tf_op jit(solution)/shard_map/all_gather | solution.py:249
  58.8 0.1 constant_dynamic-slice_fusion.2
  58.9 0.1 stack.88
  59.1 1.9 %fusion.8 = (bf16[2,640,512]{1,2,0:T(8,128)(2,1)S(1)}, bf16[2,640,512]{1,2,0:T(8,128)(2,1)}) fusion(bf16[2,12,640]{2,1,0:T(8,128)(2,1)S(1)} %reshape.95, bf16[12,512,1]{1,0,2:T(8,128)(2,1)S(1)} %reshape.102), kind=kOutput, calls=%fused_computation.15 | convolution fusion | flops 20316160 | bytes 2664448 | tf_op jit(solution)/shard_map/nqp,qh->nph/dot_general | solution.py:259
  61.0 1.0 fusion.40
  62.0 1.3 all-gather.2.cloned.1.call-done.mine_ref
  63.2 0.0 collective-permute-start
  63.2 1.2 fusion.12
  64.4 1.6 %copy.17 = f32[640,512]{1,0:T(8,128)} copy(f32[640,512]{0,1:T(8,128)S(1)} %fusion.12) | data formatting | bytes 2621440 | tf_op jit(solution)/shard_map/add | solution.py:277
  66.0 2.2 %fusion.9 = (bf16[1,1,640,1536]{2,3,1,0:T(8,128)(2,1)S(1)}, bf16[1,1,640,1536]{2,3,1,0:T(8,128)(2,1)S(1)}, bf16[1,1,640,1536]{2,3,1,0:T(8,128)(2,1)S(1)}) fusion(bf16[1,640,512]{1,2,0:T(8,128)(2,1)} %get-tuple-element.18, bf16[1,640,512]{1,2,0:T(8,128)(2,1)S(1)} %get-tuple-element.17), kind=kLoop, calls=%fused_computation.21 | loop fusion | flops 13762560 | bytes 7208960 | tf_op jit(solution)/shard_map/stack | solution.py:264
  68.3 0.0 collective-permute-done.2
  68.3 0.0 collective-permute-done.3
  68.3 0.0 collective-permute-done.1
  68.3 1.9 %select_bitcast_fusion.3 = (bf16[1,9,256,128]{3,2,1,0:T(8,128)(2,1)S(1)}, bf16[1,9,256,128]{3,2,1,0:T(8,128)(2,1)S(1)}, bf16[1,9,256,128]{3,2,1,0:T(8,128)(2,1)S(1)}, bf16[1,9,256,128]{3,2,1,0:T(8,128)(2,1)S(1)}) fusion(bf16[9,256,128]{2,1,0:T(8,128)(2,1)} %collective-permute-done.2, bf16[9,256,128]{2,1,0:T(8,128)(2,1)} %collective-permute-done.3, ...), kind=kLoop, calls=%fused_computation.30 | loop fusion | flops 3538944 | bytes 4718595 | tf_op jit(solution)/shard_map/stack | solution.py:235
  70.2 0.3 pad_maximum_fusion.6.mine_ref
  70.5 0.0 copy-start.1
  70.5 0.6 collective-permute-start.4
  71.0 0.6 copy-done.2
  71.6 3.4 %add_convert_fusion.image_ref = bf16[3,640,512]{2,1,0:T(8,128)(2,1)S(1)} fusion(bf16[1536,512,1]{1,0,2:T(8,128)(2,1)S(1)} %bitcast.151, bf16[1,1,640,1536]{2,3,1,0:T(8,128)(2,1)S(1)} %get-tuple-element.40, bf16[1,1,640,1536]{2,3,1,0:T(8,128)(2,1)S(1)} %get-tuple-element.16, bf16[1,1,640,1536]{2,3,1,0:T(8,128)(2,1)S(1)} %get-tuple-element.15, ...), kind=kOutput, calls=%fused_computation.6 | convolution fusion | flops 3027763200 | bytes 10747904 | tf_op jit(solution)/shard_map/jnpk,kg->jnpg/dot_general | solution.py:271
  75.1 0.1 fusion.38
  75.2 0.0 collective-permute-done.other_ref
  75.2 18.3 %shard_map.55 = bf16[3,640,512]{2,1,0:T(8,128)(2,1)S(1)} custom-call(s32[1]{0:T(128)} %bitcast.core_ref, bf16[3,640,512]{2,1,0:T(8,128)(2,1)S(1)} %add_convert_fusion.image_ref, bf16[4,9,256,128]{3,2,1,0:T(8,128)(2,1)} %all-gather.2.cloned.1.call-done.mine_ref, bf16[4,9,256,128]{3,2,1,0:T(8,128)(2,1)} %collective-permute-done.other_ref), custom_call_target="tpu_custom_call" | custom-call | flops 9059696640 | bytes 8650752 | tf_op jit(solution)/shard_map/pallas_call | solution.py:200
  93.5 0.1 fusion.39
  93.7 0.0 collective-permute-done.4.other_ref
  93.7 1.4 copy-done.5
  95.1 7.7 %shard_map.58 = bf16[1,4,640,128]{3,2,1,0:T(8,128)(2,1)S(1)} custom-call(s32[1]{0:T(128)} %bitcast.core_ref, bf16[1,640,512]{2,1,0:T(8,128)(2,1)S(1)} %get-tuple-element.13.image_ref, bf16[4,9,256,128]{3,2,1,0:T(8,128)(2,1)} %copy-done.1, bf16[4,9,256,128]{3,2,1,0:T(8,128)(2,1)} %copy-done.5, bf16[1,640,512]{2,1,0:T(8,128)(2,1)S(1)} %get-tuple-element.10.rest_0_), custom_call_target="tpu_custom_call" | custom-call | flops 3019898880 | bytes 6029312 | tf_op jit(solution)/shard_map/pallas_call | solution.py:200
  102.8 1.5 %collective-permute-start.11 = (bf16[1,640,128]{2,1,0:T(8,128)(2,1)S(1)}, bf16[1,640,128]{2,1,0:T(8,128)(2,1)S(1)}, u32[]{:S(2)}, u32[]{:S(2)}) collective-permute-start(bf16[1,640,128]{2,1,0:T(8,128)(2,1)S(1)} %get-tuple-element.39), channel_id=1, source_target_pairs={{0,8},{8,0},{16,24},{24,16},{1,9},{9,1},{17,25},{25,17},{2,10},{10... | collective-permute-start | bytes 491528 | tf_op jit(solution)/shard_map/ppermute | solution.py:303
  104.4 0.6 collective-permute-start.12
  105.0 1.4 collective-permute-start.13
  106.4 7.5 %shard_map.57 = bf16[1,4,640,128]{3,2,1,0:T(8,128)(2,1)S(1)} custom-call(s32[1]{0:T(128)} %bitcast.core_ref, bf16[1,640,512]{2,1,0:T(8,128)(2,1)S(1)} %get-tuple-element.14.image_ref, bf16[4,9,256,128]{3,2,1,0:T(8,128)(2,1)} %copy-done.1, bf16[4,9,256,128]{3,2,1,0:T(8,128)(2,1)} %copy-done.5, bf16[1,640,512]{2,1,0:T(8,128)(2,1)S(1)} %get-tuple-element.11.rest_0_), custom_call_target="tpu_custom_call" | custom-call | flops 3019898880 | bytes 6029312 | tf_op jit(solution)/shard_map/pallas_call | solution.py:200
  114.0 1.5 %collective-permute-start.8 = (bf16[1,640,128]{2,1,0:T(8,128)(2,1)S(1)}, bf16[1,640,128]{2,1,0:T(8,128)(2,1)S(1)}, u32[]{:S(2)}, u32[]{:S(2)}) collective-permute-start(bf16[1,640,128]{2,1,0:T(8,128)(2,1)S(1)} %get-tuple-element.36), channel_id=1, source_target_pairs={{0,8},{8,0},{16,24},{24,16},{1,9},{9,1},{17,25},{25,17},{2,10},{10... | collective-permute-start | bytes 491528 | tf_op jit(solution)/shard_map/ppermute | solution.py:303
  115.5 0.6 collective-permute-start.9
  116.1 7.5 %shard_map.56 = bf16[1,4,640,128]{3,2,1,0:T(8,128)(2,1)S(1)} custom-call(s32[1]{0:T(128)} %bitcast.core_ref, bf16[1,640,512]{2,1,0:T(8,128)(2,1)S(1)} %get-tuple-element.12.image_ref, bf16[4,9,256,128]{3,2,1,0:T(8,128)(2,1)} %copy-done.1, bf16[4,9,256,128]{3,2,1,0:T(8,128)(2,1)} %copy-done.5, bf16[1,640,512]{2,1,0:T(8,128)(2,1)S(1)} %get-tuple-element.9.rest_0_), custom_call_target="tpu_custom_call" | custom-call | flops 3019898880 | bytes 6029312 | tf_op jit(solution)/shard_map/pallas_call | solution.py:200
  123.7 0.0 collective-permute-done.11
  123.7 1.5 collective-permute-start.10
  125.1 0.0 collective-permute-done.12
  125.1 1.5 %collective-permute-start.5 = (bf16[1,640,128]{2,1,0:T(8,128)(2,1)S(1)}, bf16[1,640,128]{2,1,0:T(8,128)(2,1)S(1)}, u32[]{:S(2)}, u32[]{:S(2)}) collective-permute-start(bf16[1,640,128]{2,1,0:T(8,128)(2,1)S(1)} %get-tuple-element.33), channel_id=1, source_target_pairs={{0,8},{8,0},{16,24},{24,16},{1,9},{9,1},{17,25},{25,17},{2,10},{10... | collective-permute-start | bytes 491528 | tf_op jit(solution)/shard_map/ppermute | solution.py:303
  126.6 0.0 collective-permute-done.13
  126.6 0.6 collective-permute-start.6
  127.2 0.1 fusion.14
  127.3 0.0 collective-permute-done.8
  127.3 1.5 collective-permute-start.7
  128.8 0.0 collective-permute-done.9
  128.8 3.0 %collective-permute-done.10 = bf16[1,640,128]{2,1,0:T(8,128)(2,1)S(1)} collective-permute-done((bf16[1,640,128]{2,1,0:T(8,128)(2,1)S(1)}, bf16[1,640,128]{2,1,0:T(8,128)(2,1)S(1)}, u32[]{:S(2)}, u32[]{:S(2)}) %collective-permute-start.10) | collective-permute-done | bytes 163872 | tf_op jit(solution)/shard_map/ppermute | solution.py:303
  131.8 0.1 fusion.22
  131.9 3.1 %collective-permute-done.5 = bf16[1,640,128]{2,1,0:T(8,128)(2,1)S(1)} collective-permute-done((bf16[1,640,128]{2,1,0:T(8,128)(2,1)S(1)}, bf16[1,640,128]{2,1,0:T(8,128)(2,1)S(1)}, u32[]{:S(2)}, u32[]{:S(2)}) %collective-permute-start.5) | collective-permute-done | bytes 163872 | tf_op jit(solution)/shard_map/ppermute | solution.py:303
  135.1 0.0 collective-permute-done.6
  135.1 1.7 %collective-permute-done.7 = bf16[1,640,128]{2,1,0:T(8,128)(2,1)S(1)} collective-permute-done((bf16[1,640,128]{2,1,0:T(8,128)(2,1)S(1)}, bf16[1,640,128]{2,1,0:T(8,128)(2,1)S(1)}, u32[]{:S(2)}, u32[]{:S(2)}) %collective-permute-start.7) | collective-permute-done | bytes 163872 | tf_op jit(solution)/shard_map/ppermute | solution.py:303
  136.8 0.1 fusion.30
  136.9 2.7 %maximum_maximum_fusion = bf16[4,4,640,128]{3,2,1,0:T(8,128)(2,1)} fusion(bf16[1,1,640,128]{3,2,1,0:T(8,128)(2,1)S(1)} %get-tuple-element.28, bf16[1,1,640,128]{3,2,1,0:T(8,128)(2,1)S(1)} %get-tuple-element.24, bf16[1,1,640,128]{3,2,1,0:T(8,128)(2,1)S(1)} %get-tuple-element.20, bf16[1,1,640,128]{3,2,1,0:T(8,128)(2,1)S(1)} %get-tuple-element.29, ...), kind=kLoop, calls=%fused_computation.16 | loop fusion | flops 19660800 | bytes 4587520 | tf_op jit(solution)/shard_map/concatenate | solution.py:313
  (14 shorter events, 0.2 us)
Async XLA Ops:
  6.5 64.5 %copy-start = (bf16[3,512,512]{2,1,0:T(8,128)(2,1)S(1)}, bf16[3,512,512]{2,1,0:T(8,128)(2,1)}, u32[]{:S(2)}) copy-start(bf16[3,512,512]{2,1,0:T(8,128)(2,1)} %param.7) | copy-start | bytes 4718596
  6.5 17.0 %copy-start.3 = (bf16[4,8,4,80]{3,2,1,0:T(4,128)(2,1)S(1)}, bf16[4,8,4,80]{3,2,1,0:T(4,128)(2,1)}, u32[]{:S(2)}) copy-start(bf16[4,8,4,80]{3,2,1,0:T(4,128)(2,1)} %param.5) | copy-start | bytes 61444
  6.5 56.7 %all-gather.2.cloned.1.call-start = ((), (), s32[]{:S(2)}) async-start(), calls=%async_computation | async-start | bytes 2949120 | tf_op jit(solution)/shard_map/all_gather | solution.py:222
  10.6 57.7 %collective-permute-start.2 = (bf16[9,256,128]{2,1,0:T(8,128)(2,1)}, bf16[9,256,128]{2,1,0:T(8,128)(2,1)}, u32[]{:S(2)}, u32[]{:S(2)}) collective-permute-start(bf16[9,256,128]{2,1,0:T(8,128)(2,1)} %bitcast.17), channel_id=1, source_target_pairs={{0,16},{8,24},{16,0},{24,8},{1,17},{9,25},{17,1},{25,9},{2,18},{10... | collective-permute-start | bytes 1769480 | tf_op jit(solution)/shard_map/ppermute | solution.py:232
  13.6 54.7 %collective-permute-start.3 = (bf16[9,256,128]{2,1,0:T(8,128)(2,1)}, bf16[9,256,128]{2,1,0:T(8,128)(2,1)}, u32[]{:S(2)}, u32[]{:S(2)}) collective-permute-start(bf16[9,256,128]{2,1,0:T(8,128)(2,1)} %bitcast.17), channel_id=1, source_target_pairs={{0,24},{8,16},{16,8},{24,0},{1,25},{9,17},{17,9},{25,1},{2,26},{10... | collective-permute-start | bytes 1769480 | tf_op jit(solution)/shard_map/ppermute | solution.py:232
  15.0 53.3 %collective-permute-start.1 = (bf16[9,256,128]{2,1,0:T(8,128)(2,1)}, bf16[9,256,128]{2,1,0:T(8,128)(2,1)}, u32[]{:S(2)}, u32[]{:S(2)}) collective-permute-start(bf16[9,256,128]{2,1,0:T(8,128)(2,1)} %bitcast.17), channel_id=1, source_target_pairs={{0,8},{8,0},{16,24},{24,16},{1,9},{9,1},{17,25},{25,17},{2,10},{10... | collective-permute-start | bytes 1769480 | tf_op jit(solution)/shard_map/ppermute | solution.py:232
  23.8 35.2 %copy-start.4 = (bf16[3,4,512]{2,1,0:T(4,128)(2,1)S(1)}, bf16[3,4,512]{2,1,0:T(4,128)(2,1)}, u32[]{:S(2)}) copy-start(bf16[3,4,512]{2,1,0:T(4,128)(2,1)} %param.6) | copy-start | bytes 36868
  63.2 12.0 %collective-permute-start = (bf16[4,9,256,128]{3,2,1,0:T(8,128)(2,1)}, bf16[4,9,256,128]{3,2,1,0:T(8,128)(2,1)}, u32[]{:S(2)}, u32[]{:S(2)}) collective-permute-start(bf16[4,9,256,128]{3,2,1,0:T(8,128)(2,1)} %all-gather.2.cloned.1.call-done.mine_ref), channel_id=1, source_target_pairs={{0,1},{1,0},{2,3},{3,2},{4,5},{5,4},{6,7},{7,6},{8,9},{9,8},{10,11... | collective-permute-start | bytes 7077896 | tf_op jit(solution)/shard_map/ppermute | solution.py:245
  70.1 1.5 copy-start.2
  70.5 4.6 %copy-start.1 = (bf16[4,9,256,128]{3,2,1,0:T(8,128)(2,1)}, bf16[4,9,256,128]{3,2,1,0:T(8,128)(2,1)S(1)}, u32[]{:S(2)}) copy-start(bf16[4,9,256,128]{3,2,1,0:T(8,128)(2,1)S(1)} %pad_maximum_fusion.6.mine_ref) | copy-start | bytes 7077892
  70.5 23.2 %collective-permute-start.4 = (bf16[4,9,256,128]{3,2,1,0:T(8,128)(2,1)S(1)}, bf16[4,9,256,128]{3,2,1,0:T(8,128)(2,1)S(1)}, u32[]{:S(2)}, u32[]{:S(2)}) collective-permute-start(bf16[4,9,256,128]{3,2,1,0:T(8,128)(2,1)S(1)} %pad_maximum_fusion.6.mine_ref), channel_id=1, source_target_pairs={{0,1},{1,0},{2,3},{3,2},{4,5},{5,4},{6,7},{7,6},{8,9},{9,8},{10,11... | collective-permute-start | bytes 7077896 | tf_op jit(solution)/shard_map/ppermute | solution.py:245
  93.7 1.4 copy-start.5
  102.8 20.8 %collective-permute-start.11 = (bf16[1,640,128]{2,1,0:T(8,128)(2,1)S(1)}, bf16[1,640,128]{2,1,0:T(8,128)(2,1)S(1)}, u32[]{:S(2)}, u32[]{:S(2)}) collective-permute-start(bf16[1,640,128]{2,1,0:T(8,128)(2,1)S(1)} %get-tuple-element.39), channel_id=1, source_target_pairs={{0,8},{8,0},{16,24},{24,16},{1,9},{9,1},{17,25},{25,17},{2,10},{10... | collective-permute-start | bytes 491528 | tf_op jit(solution)/shard_map/ppermute | solution.py:303
  104.4 20.8 %collective-permute-start.12 = (bf16[1,640,128]{2,1,0:T(8,128)(2,1)S(1)}, bf16[1,640,128]{2,1,0:T(8,128)(2,1)S(1)}, u32[]{:S(2)}, u32[]{:S(2)}) collective-permute-start(bf16[1,640,128]{2,1,0:T(8,128)(2,1)S(1)} %get-tuple-element.37), channel_id=1, source_target_pairs={{0,16},{8,24},{16,0},{24,8},{1,17},{9,25},{17,1},{25,9},{2,18},{10... | collective-permute-start | bytes 491528 | tf_op jit(solution)/shard_map/ppermute | solution.py:303
  105.0 21.6 %collective-permute-start.13 = (bf16[1,640,128]{2,1,0:T(8,128)(2,1)S(1)}, bf16[1,640,128]{2,1,0:T(8,128)(2,1)S(1)}, u32[]{:S(2)}, u32[]{:S(2)}) collective-permute-start(bf16[1,640,128]{2,1,0:T(8,128)(2,1)S(1)} %get-tuple-element.38), channel_id=1, source_target_pairs={{0,24},{8,16},{16,8},{24,0},{1,25},{9,17},{17,9},{25,1},{2,26},{10... | collective-permute-start | bytes 491528 | tf_op jit(solution)/shard_map/ppermute | solution.py:303
  114.0 13.4 %collective-permute-start.8 = (bf16[1,640,128]{2,1,0:T(8,128)(2,1)S(1)}, bf16[1,640,128]{2,1,0:T(8,128)(2,1)S(1)}, u32[]{:S(2)}, u32[]{:S(2)}) collective-permute-start(bf16[1,640,128]{2,1,0:T(8,128)(2,1)S(1)} %get-tuple-element.36), channel_id=1, source_target_pairs={{0,8},{8,0},{16,24},{24,16},{1,9},{9,1},{17,25},{25,17},{2,10},{10... | collective-permute-start | bytes 491528 | tf_op jit(solution)/shard_map/ppermute | solution.py:303
  115.5 13.3 %collective-permute-start.9 = (bf16[1,640,128]{2,1,0:T(8,128)(2,1)S(1)}, bf16[1,640,128]{2,1,0:T(8,128)(2,1)S(1)}, u32[]{:S(2)}, u32[]{:S(2)}) collective-permute-start(bf16[1,640,128]{2,1,0:T(8,128)(2,1)S(1)} %get-tuple-element.34), channel_id=1, source_target_pairs={{0,16},{8,24},{16,0},{24,8},{1,17},{9,25},{17,1},{25,9},{2,18},{10... | collective-permute-start | bytes 491528 | tf_op jit(solution)/shard_map/ppermute | solution.py:303
  123.7 8.2 %collective-permute-start.10 = (bf16[1,640,128]{2,1,0:T(8,128)(2,1)S(1)}, bf16[1,640,128]{2,1,0:T(8,128)(2,1)S(1)}, u32[]{:S(2)}, u32[]{:S(2)}) collective-permute-start(bf16[1,640,128]{2,1,0:T(8,128)(2,1)S(1)} %get-tuple-element.35), channel_id=1, source_target_pairs={{0,24},{8,16},{16,8},{24,0},{1,25},{9,17},{17,9},{25,1},{2,26},{10... | collective-permute-start | bytes 491528 | tf_op jit(solution)/shard_map/ppermute | solution.py:303
  125.1 9.9 %collective-permute-start.5 = (bf16[1,640,128]{2,1,0:T(8,128)(2,1)S(1)}, bf16[1,640,128]{2,1,0:T(8,128)(2,1)S(1)}, u32[]{:S(2)}, u32[]{:S(2)}) collective-permute-start(bf16[1,640,128]{2,1,0:T(8,128)(2,1)S(1)} %get-tuple-element.33), channel_id=1, source_target_pairs={{0,8},{8,0},{16,24},{24,16},{1,9},{9,1},{17,25},{25,17},{2,10},{10... | collective-permute-start | bytes 491528 | tf_op jit(solution)/shard_map/ppermute | solution.py:303
  126.6 8.4 %collective-permute-start.6 = (bf16[1,640,128]{2,1,0:T(8,128)(2,1)S(1)}, bf16[1,640,128]{2,1,0:T(8,128)(2,1)S(1)}, u32[]{:S(2)}, u32[]{:S(2)}) collective-permute-start(bf16[1,640,128]{2,1,0:T(8,128)(2,1)S(1)} %get-tuple-element.31), channel_id=1, source_target_pairs={{0,16},{8,24},{16,0},{24,8},{1,17},{9,25},{17,1},{25,9},{2,18},{10... | collective-permute-start | bytes 491528 | tf_op jit(solution)/shard_map/ppermute | solution.py:303
  127.3 9.5 %collective-permute-start.7 = (bf16[1,640,128]{2,1,0:T(8,128)(2,1)S(1)}, bf16[1,640,128]{2,1,0:T(8,128)(2,1)S(1)}, u32[]{:S(2)}, u32[]{:S(2)}) collective-permute-start(bf16[1,640,128]{2,1,0:T(8,128)(2,1)S(1)} %get-tuple-element.32), channel_id=1, source_target_pairs={{0,24},{8,16},{16,8},{24,0},{1,25},{9,17},{17,9},{25,1},{2,26},{10... | collective-permute-start | bytes 491528 | tf_op jit(solution)/shard_map/ppermute | solution.py:303
Sparse Core Ops, SparseCore 0:
  9.2 53.9 all-gather.1

commit v3 on v2

--- a/solution.py
+++ b/solution.py
@@ -216,12 +216,6 @@
     )(*operands)
 
 
-def gather_half(weight, core):
-    half = weight.shape[2] // 2
-    mine = lax.dynamic_slice_in_dim(weight, core * half, half, 2)
-    return lax.all_gather(mine.reshape((9,) + mine.shape[2:]), "section", axis=0, tiled=False)
-
-
 def permute_half(weight, core):
     sections = lax.axis_size("section")
     section_at = lax.axis_index("section")
@@ -246,7 +240,19 @@
 
 
 def unique_frames(latents, w_in, w_time, own):
-    gathered = lax.all_gather(latents, "rows", axis=3, tiled=True)
+    size = lax.axis_size("rows")
+    row_at = lax.axis_index("rows")
+    blocks = [latents] + [
+        lax.ppermute(latents, "rows", [(i, (i + hop) % size) for i in range(size)])
+        for hop in range(1, size)
+    ]
+    gathered = jnp.concatenate(
+        [
+            lax.select_n(row_at, *[blocks[(row - sender) % size] for row in range(size)])
+            for sender in range(size)
+        ],
+        axis=3,
+    )
     flat_latents = gathered.reshape(CLIPS * LF, LATC, HS * W)
     clip = own // LF
     at = own % LF
@@ -287,7 +293,7 @@
     first = (lax.axis_index("rows") * sections + section_at) * count
     own = first + jnp.arange(count, dtype=jnp.int32)
     core = lax.axis_index("rows") % 2
-    first_halves = swap_half(gather_half(w_first, core))
+    first_halves = swap_half(permute_half(w_first, core))
     second_halves = swap_half(permute_half(w_second, core))
     framed = unique_frames(latents, w_in, w_time, own)
     cells, channels = framed.shape[2:]

time: 147 us -> 152 us (1.034)
  waiting for transfers between devices: 9.23 us -> 45.5 us
  blocking collectives: 28.1 us -> 0 us
  between operations: 25 us -> 11.3 us
  starting transfers between devices: 15.8 us -> 28.2 us
  local copies, waits for them, and re-layouts: 13.4 us -> 10.4 us
  other arithmetic: 8.62 us -> 10.6 us
    ppermute x3 -> x6, waiting for transfers between devices: 0.01 us -> 37.6 us  [permute_half(): lax.ppermute(own, 'section', [(i, i ^ hop) for i in range(sections)])]
    all_gather x1 -> x0, blocking collectives: 28.1 us -> none  [unique_frames(): gathered = lax.all_gather(latents, 'rows', axis=3, tiled=True)]
    ppermute x0 -> x7, starting transfers between devices: none -> 9.45 us  [unique_frames(): lax.ppermute(latents, 'rows', [(i, (i + hop) % size) for i in range(size)])]
    ppermute x3 -> x6, starting transfers between devices: 4.46 us -> 8 us  [permute_half(): lax.ppermute(own, 'section', [(i, i ^ hop) for i in range(sections)])]
    another operation x2 -> x4, other arithmetic: 2.15 us -> 5.33 us  [permute_half(): jnp.stack([lax.select_n(section_at, *[parts[sender ^ s] for s in range(se...]
    all_gather x1 -> x0, local copies, waits for them, and re-layouts: 3.08 us -> none  [unique_frames(): gathered = lax.all_gather(latents, 'rows', axis=3, tiled=True)]
    dynamic_slice x2 -> x0, local copies, waits for them, and re-layouts: 2.17 us -> none  [the longest x1 2.09 us: gather_half(): mine = lax.dynamic_slice_in_dim(weight, core * half, half, 2)]
  transfers between devices with their start and end apart: 15 -> 24, of which waited for: 4 -> 8; matrix products, arithmetic and copies ran while one was open for 14% -> 13% of each run, Pallas kernels for 23% -> 22%
where the time goes in v3:
time: 152 us
  waiting for transfers between devices  45.5 us (30%)
  Pallas kernels  41.2 us (27%)
  starting transfers between devices  28.2 us (19%)
  between operations  11.3 us (7%)
  other arithmetic  10.6 us (7%)
  local copies, waits for them, and re-layouts  10.4 us (7%)
  matrix products  4.31 us (3%)
    pallas_call x4, Pallas kernels, norm_conv(): pl.pallas_call(functools.partial(norm_conv_kernel, split), grid=(frames,)...  41.2 us
    ppermute x6, waiting for transfers between devices, permute_half(): lax.ppermute(own, 'section', [(i, i ^ hop) for i in range(sections)])  37.6 us
    ppermute x9, starting transfers between devices, per_device_frames(): lax.ppermute(part, 'section', [(i, i ^ hop) for i in range(sections)])  10.7 us
    ppermute x7, starting transfers between devices, unique_frames(): lax.ppermute(latents, 'rows', [(i, (i + hop) % size) for i in range(size)])  9.45 us
    ppermute x6, starting transfers between devices, permute_half(): lax.ppermute(own, 'section', [(i, i ^ hop) for i in range(sections)])  8 us
    ppermute x9, waiting for transfers between devices, per_device_frames(): lax.ppermute(part, 'section', [(i, i ^ hop) for i in range(sections)])  7.87 us
    another operation x4, other arithmetic, permute_half(): jnp.stack([lax.select_n(section_at, *[parts[sender ^ s] for s in range(se...  5.33 us
    dot_general x1, matrix products, unique_frames(): jnp.einsum('jnpk,kg->jnpg', stacked, w_time.reshape(-1, w_time.shape[2]),...  3.42 us
  transfers between devices with their start and end apart: 24, of which 8 were waited for; matrix products, arithmetic and copies ran while one was open for 13% of the time, Pallas kernels for 22%

profile of v3, /device:TPU:0, one launch (start us, length us, event | category | flops | bytes accessed | tf_op | source)
XLA Modules:
  0.0 151.6 jit_solution(6258806846775664117)
XLA Ops:
  0.0 4.5 %collective-permute-start.6 = (bf16[4,8,4,80]{3,2,1,0:T(4,128)(2,1)}, bf16[4,8,4,80]{3,2,1,0:T(4,128)(2,1)S(1)}, u32[]{:S(2)}, u32[]{:S(2)}) collective-permute-start(bf16[4,8,4,80]{3,2,1,0:T(4,128)(2,1)} %param.5), channel_id=1, source_target_pairs={{0,7},{1,0},{2,1},{3,2},{4,3},{5,4},{6,5},{7,6},{8,15},{9,8},{10,9... | collective-permute-start | bytes 61448 | tf_op jit(solution)/shard_map/ppermute | solution.py:246
  4.5 0.0 collective-permute-start.4
  4.5 1.0 collective-permute-start.5
  5.5 1.1 collective-permute-start.2
  6.6 0.6 collective-permute-start.3
  7.2 0.1 add_add_fusion
  7.3 0.1 maximum_add_fusion
  7.4 1.1 constant_dynamic-slice_fusion.1
  8.5 1.9 %constant_dynamic-slice_fusion = bf16[3,3,256,128]{3,2,1,0:T(8,128)(2,1)} fusion(bf16[3,3,512,128]{3,2,1,0:T(8,128)(2,1)} %param.9, s32[]{:T(128)S(6)} %select_n.773), kind=kLoop, calls=%fused_computation.95 | loop fusion | bytes 1179652 | tf_op jit(solution)/shard_map/dynamic_slice | solution.py:223
  10.4 0.1 add.121
  10.5 1.0 collective-permute-start
  11.5 0.0 collective-permute-done.4
  11.5 1.2 collective-permute-start.1
  12.7 0.7 fusion.41
  20.8 0.7 reshape.106
  25.2 1.6 %collective-permute-start.8 = (bf16[9,256,128]{2,1,0:T(8,128)(2,1)S(1)}, bf16[9,256,128]{2,1,0:T(8,128)(2,1)S(1)}, u32[]{:S(2)}, u32[]{:S(2)}) collective-permute-start(bf16[9,256,128]{2,1,0:T(8,128)(2,1)S(1)} %bitcast.180), channel_id=1, source_target_pairs={{0,16},{8,24},{16,0},{24,8},{1,17},{9,25},{17,1},{25,9},{2,18},{10... | collective-permute-start | bytes 1769480 | tf_op jit(solution)/shard_map/ppermute | solution.py:226
  26.8 1.4 collective-permute-start.9
  28.2 0.5 collective-permute-start.7
  28.7 1.5 %collective-permute-start.12 = (bf16[9,256,128]{2,1,0:T(8,128)(2,1)}, bf16[9,256,128]{2,1,0:T(8,128)(2,1)}, u32[]{:S(2)}, u32[]{:S(2)}) collective-permute-start(bf16[9,256,128]{2,1,0:T(8,128)(2,1)} %bitcast.21), channel_id=1, source_target_pairs={{0,16},{8,24},{16,0},{24,8},{1,17},{9,25},{17,1},{25,9},{2,18},{10... | collective-permute-start | bytes 1769480 | tf_op jit(solution)/shard_map/ppermute | solution.py:226
  30.3 1.4 collective-permute-start.13
  31.7 0.1 select_select_fusion
  31.8 0.4 concatenate.29
  32.4 0.9 fusion.8
  33.3 1.0 fusion.40
  34.2 19.8 %collective-permute-done.8 = bf16[9,256,128]{2,1,0:T(8,128)(2,1)S(1)} collective-permute-done((bf16[9,256,128]{2,1,0:T(8,128)(2,1)S(1)}, bf16[9,256,128]{2,1,0:T(8,128)(2,1)S(1)}, u32[]{:S(2)}, u32[]{:S(2)}) %collective-permute-start.8) | collective-permute-done | bytes 589856 | tf_op jit(solution)/shard_map/ppermute | solution.py:226
  54.0 1.5 collective-permute-start.11
  55.5 0.2 collective-permute-done.7
  55.7 1.5 select_bitcast_fusion.7
  57.2 1.7 %pad_maximum_fusion.6.mine_ref = bf16[4,9,256,128]{3,2,1,0:T(8,128)(2,1)} fusion(bf16[1,9,256,128]{3,2,1,0:T(8,128)(2,1)S(1)} %get-tuple-element.10, bf16[1,9,256,128]{3,2,1,0:T(8,128)(2,1)S(1)} %get-tuple-element.11, bf16[1,9,256,128]{3,2,1,0:T(8,128)(2,1)S(1)} %get-tuple-element.12, bf16[1,9,256,128]{3,2,1,0:T(8,128)(2,1)S(1)} %get-tuple-element.9), kind=kLoop, calls=%fused_computation.20 | loop fusion | flops 3538944 | bytes 4718592 | tf_op jit(solution)/shard_map/stack | solution.py:229
  58.9 0.1 fusion.12
  59.0 1.5 copy.9
  60.5 2.1 %fusion.9 = (bf16[1,1,640,1536]{2,3,1,0:T(8,128)(2,1)S(1)}, bf16[1,1,640,1536]{2,3,1,0:T(8,128)(2,1)S(1)}, bf16[1,1,640,1536]{2,3,1,0:T(8,128)(2,1)S(1)}) fusion(bf16[1,640,512]{1,2,0:T(8,128)(2,1)} %get-tuple-element.22, bf16[1,640,512]{1,2,0:T(8,128)(2,1)S(1)} %get-tuple-element.21), kind=kLoop, calls=%fused_computation.22 | loop fusion | flops 13762560 | bytes 7208960 | tf_op jit(solution)/shard_map/stack | solution.py:270
  62.5 16.4 %collective-permute-done.12 = bf16[9,256,128]{2,1,0:T(8,128)(2,1)} collective-permute-done((bf16[9,256,128]{2,1,0:T(8,128)(2,1)}, bf16[9,256,128]{2,1,0:T(8,128)(2,1)}, u32[]{:S(2)}, u32[]{:S(2)}) %collective-permute-start.12) | collective-permute-done | bytes 589856 | tf_op jit(solution)/shard_map/ppermute | solution.py:226
  79.0 1.3 collective-permute-done.11
  80.2 1.8 %select_bitcast_fusion.3 = (bf16[1,9,256,128]{3,2,1,0:T(8,128)(2,1)S(1)}, bf16[1,9,256,128]{3,2,1,0:T(8,128)(2,1)S(1)}, bf16[1,9,256,128]{3,2,1,0:T(8,128)(2,1)S(1)}, bf16[1,9,256,128]{3,2,1,0:T(8,128)(2,1)S(1)}) fusion(bf16[9,256,128]{2,1,0:T(8,128)(2,1)} %collective-permute-done.12, bf16[9,256,128]{2,1,0:T(8,128)(2,1)} %collective-permute-done.13, ...), kind=kLoop, calls=%fused_computation.31 | loop fusion | flops 3538944 | bytes 4718595 | tf_op jit(solution)/shard_map/stack | solution.py:229
  82.1 0.3 pad_maximum_fusion.7.mine_ref
  82.4 0.1 collective-permute-start.14
  82.5 1.1 copy-done.2
  83.6 3.4 %add_convert_fusion.image_ref = bf16[3,640,512]{2,1,0:T(8,128)(2,1)S(1)} fusion(bf16[1536,512,1]{1,0,2:T(8,128)(2,1)S(1)} %bitcast.179, bf16[1,1,640,1536]{2,3,1,0:T(8,128)(2,1)S(1)} %get-tuple-element.44, bf16[1,1,640,1536]{2,3,1,0:T(8,128)(2,1)S(1)} %get-tuple-element.20, bf16[1,1,640,1536]{2,3,1,0:T(8,128)(2,1)S(1)} %get-tuple-element.19, ...), kind=kOutput, calls=%fused_computation.6 | convolution fusion | flops 3027763200 | bytes 10747904 | tf_op jit(solution)/shard_map/jnpk,kg->jnpg/dot_general | solution.py:277
  87.0 0.1 fusion.38
  87.1 18.5 %shard_map.55 = bf16[3,640,512]{2,1,0:T(8,128)(2,1)S(1)} custom-call(s32[1]{0:T(128)} %bitcast.core_ref, bf16[3,640,512]{2,1,0:T(8,128)(2,1)S(1)} %add_convert_fusion.image_ref, bf16[4,9,256,128]{3,2,1,0:T(8,128)(2,1)} %pad_maximum_fusion.6.mine_ref, bf16[4,9,256,128]{3,2,1,0:T(8,128)(2,1)} %collective-permute-done.10.other_ref), custom_call_target="tpu_custom_call" | custom-call | flops 9059696640 | bytes 8650752 | tf_op jit(solution)/shard_map/pallas_call | solution.py:200
  105.6 0.1 fusion.39
  105.8 0.0 copy-start.4
  105.8 1.4 copy-done.4
  107.2 7.5 %shard_map.58 = bf16[1,4,640,128]{3,2,1,0:T(8,128)(2,1)S(1)} custom-call(s32[1]{0:T(128)} %bitcast.core_ref, bf16[1,640,512]{2,1,0:T(8,128)(2,1)S(1)} %get-tuple-element.17.image_ref, bf16[4,9,256,128]{3,2,1,0:T(8,128)(2,1)} %copy-done.1, bf16[4,9,256,128]{3,2,1,0:T(8,128)(2,1)} %copy-done.4, bf16[1,640,512]{2,1,0:T(8,128)(2,1)S(1)} %get-tuple-element.14.rest_0_), custom_call_target="tpu_custom_call" | custom-call | flops 3019898880 | bytes 6029312 | tf_op jit(solution)/shard_map/pallas_call | solution.py:200
  114.7 1.6 %collective-permute-start.21 = (bf16[1,640,128]{2,1,0:T(8,128)(2,1)S(1)}, bf16[1,640,128]{2,1,0:T(8,128)(2,1)S(1)}, u32[]{:S(2)}, u32[]{:S(2)}) collective-permute-start(bf16[1,640,128]{2,1,0:T(8,128)(2,1)S(1)} %get-tuple-element.43), channel_id=1, source_target_pairs={{0,8},{8,0},{16,24},{24,16},{1,9},{9,1},{17,25},{25,17},{2,10},{10... | collective-permute-start | bytes 491528 | tf_op jit(solution)/shard_map/ppermute | solution.py:309
  116.3 1.5 %collective-permute-start.22 = (bf16[1,640,128]{2,1,0:T(8,128)(2,1)S(1)}, bf16[1,640,128]{2,1,0:T(8,128)(2,1)S(1)}, u32[]{:S(2)}, u32[]{:S(2)}) collective-permute-start(bf16[1,640,128]{2,1,0:T(8,128)(2,1)S(1)} %get-tuple-element.41), channel_id=1, source_target_pairs={{0,16},{8,24},{16,0},{24,8},{1,17},{9,25},{17,1},{25,9},{2,18},{10... | collective-permute-start | bytes 491528 | tf_op jit(solution)/shard_map/ppermute | solution.py:309
  117.8 0.5 collective-permute-start.23
  118.3 7.5 %shard_map.57 = bf16[1,4,640,128]{3,2,1,0:T(8,128)(2,1)S(1)} custom-call(s32[1]{0:T(128)} %bitcast.core_ref, bf16[1,640,512]{2,1,0:T(8,128)(2,1)S(1)} %get-tuple-element.18.image_ref, bf16[4,9,256,128]{3,2,1,0:T(8,128)(2,1)} %copy-done.1, bf16[4,9,256,128]{3,2,1,0:T(8,128)(2,1)} %copy-done.4, bf16[1,640,512]{2,1,0:T(8,128)(2,1)S(1)} %get-tuple-element.15.rest_0_), custom_call_target="tpu_custom_call" | custom-call | flops 3019898880 | bytes 6029312 | tf_op jit(solution)/shard_map/pallas_call | solution.py:200
  125.9 1.6 %collective-permute-start.18 = (bf16[1,640,128]{2,1,0:T(8,128)(2,1)S(1)}, bf16[1,640,128]{2,1,0:T(8,128)(2,1)S(1)}, u32[]{:S(2)}, u32[]{:S(2)}) collective-permute-start(bf16[1,640,128]{2,1,0:T(8,128)(2,1)S(1)} %get-tuple-element.40), channel_id=1, source_target_pairs={{0,8},{8,0},{16,24},{24,16},{1,9},{9,1},{17,25},{25,17},{2,10},{10... | collective-permute-start | bytes 491528 | tf_op jit(solution)/shard_map/ppermute | solution.py:309
  127.4 1.5 %collective-permute-start.19 = (bf16[1,640,128]{2,1,0:T(8,128)(2,1)S(1)}, bf16[1,640,128]{2,1,0:T(8,128)(2,1)S(1)}, u32[]{:S(2)}, u32[]{:S(2)}) collective-permute-start(bf16[1,640,128]{2,1,0:T(8,128)(2,1)S(1)} %get-tuple-element.38), channel_id=1, source_target_pairs={{0,16},{8,24},{16,0},{24,8},{1,17},{9,25},{17,1},{25,9},{2,18},{10... | collective-permute-start | bytes 491528 | tf_op jit(solution)/shard_map/ppermute | solution.py:309
  128.9 7.7 %shard_map.56 = bf16[1,4,640,128]{3,2,1,0:T(8,128)(2,1)S(1)} custom-call(s32[1]{0:T(128)} %bitcast.core_ref, bf16[1,640,512]{2,1,0:T(8,128)(2,1)S(1)} %get-tuple-element.16.image_ref, bf16[4,9,256,128]{3,2,1,0:T(8,128)(2,1)} %copy-done.1, bf16[4,9,256,128]{3,2,1,0:T(8,128)(2,1)} %copy-done.4, bf16[1,640,512]{2,1,0:T(8,128)(2,1)S(1)} %get-tuple-element.13.rest_0_), custom_call_target="tpu_custom_call" | custom-call | flops 3019898880 | bytes 6029312 | tf_op jit(solution)/shard_map/pallas_call | solution.py:200
  136.7 0.5 collective-permute-start.20
  137.3 1.5 collective-permute-start.15
  138.8 1.5 %collective-permute-start.16 = (bf16[1,640,128]{2,1,0:T(8,128)(2,1)S(1)}, bf16[1,640,128]{2,1,0:T(8,128)(2,1)S(1)}, u32[]{:S(2)}, u32[]{:S(2)}) collective-permute-start(bf16[1,640,128]{2,1,0:T(8,128)(2,1)S(1)} %get-tuple-element.35), channel_id=1, source_target_pairs={{0,16},{8,24},{16,0},{24,8},{1,17},{9,25},{17,1},{25,9},{2,18},{10... | collective-permute-start | bytes 491528 | tf_op jit(solution)/shard_map/ppermute | solution.py:309
  140.3 0.1 fusion.14
  140.4 0.5 collective-permute-start.17
  140.9 4.0 %collective-permute-done.20 = bf16[1,640,128]{2,1,0:T(8,128)(2,1)S(1)} collective-permute-done((bf16[1,640,128]{2,1,0:T(8,128)(2,1)S(1)}, bf16[1,640,128]{2,1,0:T(8,128)(2,1)S(1)}, u32[]{:S(2)}, u32[]{:S(2)}) %collective-permute-start.20) | collective-permute-done | bytes 163872 | tf_op jit(solution)/shard_map/ppermute | solution.py:309
  144.9 0.1 fusion.22
  145.0 1.1 collective-permute-done.15
  146.1 1.0 collective-permute-done.16
  147.1 1.8 %collective-permute-done.17 = bf16[1,640,128]{2,1,0:T(8,128)(2,1)S(1)} collective-permute-done((bf16[1,640,128]{2,1,0:T(8,128)(2,1)S(1)}, bf16[1,640,128]{2,1,0:T(8,128)(2,1)S(1)}, u32[]{:S(2)}, u32[]{:S(2)}) %collective-permute-start.17) | collective-permute-done | bytes 163872 | tf_op jit(solution)/shard_map/ppermute | solution.py:309
  148.9 0.1 fusion.30
  149.0 2.7 %maximum_maximum_fusion = bf16[4,4,640,128]{3,2,1,0:T(8,128)(2,1)} fusion(bf16[1,1,640,128]{3,2,1,0:T(8,128)(2,1)S(1)} %get-tuple-element.32, bf16[1,1,640,128]{3,2,1,0:T(8,128)(2,1)S(1)} %get-tuple-element.28, bf16[1,1,640,128]{3,2,1,0:T(8,128)(2,1)S(1)} %get-tuple-element.24, bf16[1,1,640,128]{3,2,1,0:T(8,128)(2,1)S(1)} %get-tuple-element.33, ...), kind=kLoop, calls=%fused_computation.16 | loop fusion | flops 19660800 | bytes 4587520 | tf_op jit(solution)/shard_map/concatenate | solution.py:319
  (33 shorter events, 0.3 us)
Async XLA Ops:
  0.0 82.5 %copy-start = (bf16[3,512,512]{2,1,0:T(8,128)(2,1)S(1)}, bf16[3,512,512]{2,1,0:T(8,128)(2,1)}, u32[]{:S(2)}) copy-start(bf16[3,512,512]{2,1,0:T(8,128)(2,1)} %param.7) | copy-start | bytes 4718596
  0.0 31.7 %copy-start.3 = (bf16[4,8,4,80]{3,2,1,0:T(4,128)(2,1)S(1)}, bf16[4,8,4,80]{3,2,1,0:T(4,128)(2,1)}, u32[]{:S(2)}) copy-start(bf16[4,8,4,80]{3,2,1,0:T(4,128)(2,1)} %param.5) | copy-start | bytes 61444
  0.0 10.5 %collective-permute-start.6 = (bf16[4,8,4,80]{3,2,1,0:T(4,128)(2,1)}, bf16[4,8,4,80]{3,2,1,0:T(4,128)(2,1)S(1)}, u32[]{:S(2)}, u32[]{:S(2)}) collective-permute-start(bf16[4,8,4,80]{3,2,1,0:T(4,128)(2,1)} %param.5), channel_id=1, source_target_pairs={{0,7},{1,0},{2,1},{3,2},{4,3},{5,4},{6,5},{7,6},{8,15},{9,8},{10,9... | collective-permute-start | bytes 61448 | tf_op jit(solution)/shard_map/ppermute | solution.py:246
  4.5 7.0 %collective-permute-start.4 = (bf16[4,8,4,80]{3,2,1,0:T(4,128)(2,1)}, bf16[4,8,4,80]{3,2,1,0:T(4,128)(2,1)S(1)}, u32[]{:S(2)}, u32[]{:S(2)}) collective-permute-start(bf16[4,8,4,80]{3,2,1,0:T(4,128)(2,1)} %param.5), channel_id=1, source_target_pairs={{0,5},{1,6},{2,7},{3,0},{4,1},{5,2},{6,3},{7,4},{8,13},{9,14},{10,... | collective-permute-start | bytes 61448 | tf_op jit(solution)/shard_map/ppermute | solution.py:246
  4.5 20.7 %collective-permute-start.5 = (bf16[4,8,4,80]{3,2,1,0:T(4,128)(2,1)}, bf16[4,8,4,80]{3,2,1,0:T(4,128)(2,1)S(1)}, u32[]{:S(2)}, u32[]{:S(2)}) collective-permute-start(bf16[4,8,4,80]{3,2,1,0:T(4,128)(2,1)} %param.5), channel_id=1, source_target_pairs={{0,6},{1,7},{2,0},{3,1},{4,2},{5,3},{6,4},{7,5},{8,14},{9,15},{10,... | collective-permute-start | bytes 61448 | tf_op jit(solution)/shard_map/ppermute | solution.py:246
  5.5 21.3 %collective-permute-start.2 = (bf16[4,8,4,80]{3,2,1,0:T(4,128)(2,1)}, bf16[4,8,4,80]{3,2,1,0:T(4,128)(2,1)S(1)}, u32[]{:S(2)}, u32[]{:S(2)}) collective-permute-start(bf16[4,8,4,80]{3,2,1,0:T(4,128)(2,1)} %param.5), channel_id=1, source_target_pairs={{0,3},{1,4},{2,5},{3,6},{4,7},{5,0},{6,1},{7,2},{8,11},{9,12},{10,... | collective-permute-start | bytes 61448 | tf_op jit(solution)/shard_map/ppermute | solution.py:246
  6.6 21.6 %collective-permute-start.3 = (bf16[4,8,4,80]{3,2,1,0:T(4,128)(2,1)}, bf16[4,8,4,80]{3,2,1,0:T(4,128)(2,1)S(1)}, u32[]{:S(2)}, u32[]{:S(2)}) collective-permute-start(bf16[4,8,4,80]{3,2,1,0:T(4,128)(2,1)} %param.5), channel_id=1, source_target_pairs={{0,4},{1,5},{2,6},{3,7},{4,0},{5,1},{6,2},{7,3},{8,12},{9,13},{10,... | collective-permute-start | bytes 61448 | tf_op jit(solution)/shard_map/ppermute | solution.py:246
  10.5 18.2 %collective-permute-start = (bf16[4,8,4,80]{3,2,1,0:T(4,128)(2,1)}, bf16[4,8,4,80]{3,2,1,0:T(4,128)(2,1)S(1)}, u32[]{:S(2)}, u32[]{:S(2)}) collective-permute-start(bf16[4,8,4,80]{3,2,1,0:T(4,128)(2,1)} %param.5), channel_id=1, source_target_pairs={{0,1},{1,2},{2,3},{3,4},{4,5},{5,6},{6,7},{7,0},{8,9},{9,10},{10,1... | collective-permute-start | bytes 61448 | tf_op jit(solution)/shard_map/ppermute | solution.py:246
  11.5 18.7 %collective-permute-start.1 = (bf16[4,8,4,80]{3,2,1,0:T(4,128)(2,1)}, bf16[4,8,4,80]{3,2,1,0:T(4,128)(2,1)S(1)}, u32[]{:S(2)}, u32[]{:S(2)}) collective-permute-start(bf16[4,8,4,80]{3,2,1,0:T(4,128)(2,1)} %param.5), channel_id=1, source_target_pairs={{0,2},{1,3},{2,4},{3,5},{4,6},{5,7},{6,0},{7,1},{8,10},{9,11},{10,... | collective-permute-start | bytes 61448 | tf_op jit(solution)/shard_map/ppermute | solution.py:246
  25.2 28.8 %collective-permute-start.8 = (bf16[9,256,128]{2,1,0:T(8,128)(2,1)S(1)}, bf16[9,256,128]{2,1,0:T(8,128)(2,1)S(1)}, u32[]{:S(2)}, u32[]{:S(2)}) collective-permute-start(bf16[9,256,128]{2,1,0:T(8,128)(2,1)S(1)} %bitcast.180), channel_id=1, source_target_pairs={{0,16},{8,24},{16,0},{24,8},{1,17},{9,25},{17,1},{25,9},{2,18},{10... | collective-permute-start | bytes 1769480 | tf_op jit(solution)/shard_map/ppermute | solution.py:226
  26.8 28.7 %collective-permute-start.9 = (bf16[9,256,128]{2,1,0:T(8,128)(2,1)S(1)}, bf16[9,256,128]{2,1,0:T(8,128)(2,1)}, u32[]{:S(2)}, u32[]{:S(2)}) collective-permute-start(bf16[9,256,128]{2,1,0:T(8,128)(2,1)S(1)} %bitcast.181), channel_id=1, source_target_pairs={{0,24},{8,16},{16,8},{24,0},{1,25},{9,17},{17,9},{25,1},{2,26},{10... | collective-permute-start | bytes 1769480 | tf_op jit(solution)/shard_map/ppermute | solution.py:226
  28.2 27.5 %collective-permute-start.7 = (bf16[9,256,128]{2,1,0:T(8,128)(2,1)S(1)}, bf16[9,256,128]{2,1,0:T(8,128)(2,1)}, u32[]{:S(2)}, u32[]{:S(2)}) collective-permute-start(bf16[9,256,128]{2,1,0:T(8,128)(2,1)S(1)} %bitcast.182), channel_id=1, source_target_pairs={{0,8},{8,0},{16,24},{24,16},{1,9},{9,1},{17,25},{25,17},{2,10},{10... | collective-permute-start | bytes 1769480 | tf_op jit(solution)/shard_map/ppermute | solution.py:226
  28.7 50.2 %collective-permute-start.12 = (bf16[9,256,128]{2,1,0:T(8,128)(2,1)}, bf16[9,256,128]{2,1,0:T(8,128)(2,1)}, u32[]{:S(2)}, u32[]{:S(2)}) collective-permute-start(bf16[9,256,128]{2,1,0:T(8,128)(2,1)} %bitcast.21), channel_id=1, source_target_pairs={{0,16},{8,24},{16,0},{24,8},{1,17},{9,25},{17,1},{25,9},{2,18},{10... | collective-permute-start | bytes 1769480 | tf_op jit(solution)/shard_map/ppermute | solution.py:226
  30.3 48.7 %collective-permute-start.13 = (bf16[9,256,128]{2,1,0:T(8,128)(2,1)}, bf16[9,256,128]{2,1,0:T(8,128)(2,1)}, u32[]{:S(2)}, u32[]{:S(2)}) collective-permute-start(bf16[9,256,128]{2,1,0:T(8,128)(2,1)} %bitcast.21), channel_id=1, source_target_pairs={{0,24},{8,16},{16,8},{24,0},{1,25},{9,17},{17,9},{25,1},{2,26},{10... | collective-permute-start | bytes 1769480 | tf_op jit(solution)/shard_map/ppermute | solution.py:226
  54.0 26.2 %collective-permute-start.11 = (bf16[9,256,128]{2,1,0:T(8,128)(2,1)}, bf16[9,256,128]{2,1,0:T(8,128)(2,1)}, u32[]{:S(2)}, u32[]{:S(2)}) collective-permute-start(bf16[9,256,128]{2,1,0:T(8,128)(2,1)} %bitcast.21), channel_id=1, source_target_pairs={{0,8},{8,0},{16,24},{24,16},{1,9},{9,1},{17,25},{25,17},{2,10},{10... | collective-permute-start | bytes 1769480 | tf_op jit(solution)/shard_map/ppermute | solution.py:226
  58.9 28.3 %collective-permute-start.10 = (bf16[4,9,256,128]{3,2,1,0:T(8,128)(2,1)}, bf16[4,9,256,128]{3,2,1,0:T(8,128)(2,1)}, u32[]{:S(2)}, u32[]{:S(2)}) collective-permute-start(bf16[4,9,256,128]{3,2,1,0:T(8,128)(2,1)} %pad_maximum_fusion.6.mine_ref), channel_id=1, source_target_pairs={{0,1},{1,0},{2,3},{3,2},{4,5},{5,4},{6,7},{7,6},{8,9},{9,8},{10,11... | collective-permute-start | bytes 7077896 | tf_op jit(solution)/shard_map/ppermute | solution.py:239
  82.1 1.5 copy-start.2
  82.4 4.6 %copy-start.1 = (bf16[4,9,256,128]{3,2,1,0:T(8,128)(2,1)}, bf16[4,9,256,128]{3,2,1,0:T(8,128)(2,1)S(1)}, u32[]{:S(2)}) copy-start(bf16[4,9,256,128]{3,2,1,0:T(8,128)(2,1)S(1)} %pad_maximum_fusion.7.mine_ref) | copy-start | bytes 7077892
  82.4 23.4 %collective-permute-start.14 = (bf16[4,9,256,128]{3,2,1,0:T(8,128)(2,1)S(1)}, bf16[4,9,256,128]{3,2,1,0:T(8,128)(2,1)S(1)}, u32[]{:S(2)}, u32[]{:S(2)}) collective-permute-start(bf16[4,9,256,128]{3,2,1,0:T(8,128)(2,1)S(1)} %pad_maximum_fusion.7.mine_ref), channel_id=1, source_target_pairs={{0,1},{1,0},{2,3},{3,2},{4,5},{5,4},{6,7},{7,6},{8,9},{9,8},{10,11... | collective-permute-start | bytes 7077896 | tf_op jit(solution)/shard_map/ppermute | solution.py:239
  105.8 1.4 copy-start.4
  114.7 22.0 %collective-permute-start.21 = (bf16[1,640,128]{2,1,0:T(8,128)(2,1)S(1)}, bf16[1,640,128]{2,1,0:T(8,128)(2,1)S(1)}, u32[]{:S(2)}, u32[]{:S(2)}) collective-permute-start(bf16[1,640,128]{2,1,0:T(8,128)(2,1)S(1)} %get-tuple-element.43), channel_id=1, source_target_pairs={{0,8},{8,0},{16,24},{24,16},{1,9},{9,1},{17,25},{25,17},{2,10},{10... | collective-permute-start | bytes 491528 | tf_op jit(solution)/shard_map/ppermute | solution.py:309
  116.3 21.0 %collective-permute-start.22 = (bf16[1,640,128]{2,1,0:T(8,128)(2,1)S(1)}, bf16[1,640,128]{2,1,0:T(8,128)(2,1)S(1)}, u32[]{:S(2)}, u32[]{:S(2)}) collective-permute-start(bf16[1,640,128]{2,1,0:T(8,128)(2,1)S(1)} %get-tuple-element.41), channel_id=1, source_target_pairs={{0,16},{8,24},{16,0},{24,8},{1,17},{9,25},{17,1},{25,9},{2,18},{10... | collective-permute-start | bytes 491528 | tf_op jit(solution)/shard_map/ppermute | solution.py:309
  117.8 21.0 %collective-permute-start.23 = (bf16[1,640,128]{2,1,0:T(8,128)(2,1)S(1)}, bf16[1,640,128]{2,1,0:T(8,128)(2,1)S(1)}, u32[]{:S(2)}, u32[]{:S(2)}) collective-permute-start(bf16[1,640,128]{2,1,0:T(8,128)(2,1)S(1)} %get-tuple-element.42), channel_id=1, source_target_pairs={{0,24},{8,16},{16,8},{24,0},{1,25},{9,17},{17,9},{25,1},{2,26},{10... | collective-permute-start | bytes 491528 | tf_op jit(solution)/shard_map/ppermute | solution.py:309
  125.9 14.5 %collective-permute-start.18 = (bf16[1,640,128]{2,1,0:T(8,128)(2,1)S(1)}, bf16[1,640,128]{2,1,0:T(8,128)(2,1)S(1)}, u32[]{:S(2)}, u32[]{:S(2)}) collective-permute-start(bf16[1,640,128]{2,1,0:T(8,128)(2,1)S(1)} %get-tuple-element.40), channel_id=1, source_target_pairs={{0,8},{8,0},{16,24},{24,16},{1,9},{9,1},{17,25},{25,17},{2,10},{10... | collective-permute-start | bytes 491528 | tf_op jit(solution)/shard_map/ppermute | solution.py:309
  127.4 13.5 %collective-permute-start.19 = (bf16[1,640,128]{2,1,0:T(8,128)(2,1)S(1)}, bf16[1,640,128]{2,1,0:T(8,128)(2,1)S(1)}, u32[]{:S(2)}, u32[]{:S(2)}) collective-permute-start(bf16[1,640,128]{2,1,0:T(8,128)(2,1)S(1)} %get-tuple-element.38), channel_id=1, source_target_pairs={{0,16},{8,24},{16,0},{24,8},{1,17},{9,25},{17,1},{25,9},{2,18},{10... | collective-permute-start | bytes 491528 | tf_op jit(solution)/shard_map/ppermute | solution.py:309
  136.7 8.2 %collective-permute-start.20 = (bf16[1,640,128]{2,1,0:T(8,128)(2,1)S(1)}, bf16[1,640,128]{2,1,0:T(8,128)(2,1)S(1)}, u32[]{:S(2)}, u32[]{:S(2)}) collective-permute-start(bf16[1,640,128]{2,1,0:T(8,128)(2,1)S(1)} %get-tuple-element.39), channel_id=1, source_target_pairs={{0,24},{8,16},{16,8},{24,0},{1,25},{9,17},{17,9},{25,1},{2,26},{10... | collective-permute-start | bytes 491528 | tf_op jit(solution)/shard_map/ppermute | solution.py:309
  137.3 8.9 %collective-permute-start.15 = (bf16[1,640,128]{2,1,0:T(8,128)(2,1)S(1)}, bf16[1,640,128]{2,1,0:T(8,128)(2,1)S(1)}, u32[]{:S(2)}, u32[]{:S(2)}) collective-permute-start(bf16[1,640,128]{2,1,0:T(8,128)(2,1)S(1)} %get-tuple-element.37), channel_id=1, source_target_pairs={{0,8},{8,0},{16,24},{24,16},{1,9},{9,1},{17,25},{25,17},{2,10},{10... | collective-permute-start | bytes 491528 | tf_op jit(solution)/shard_map/ppermute | solution.py:309
  138.8 8.3 %collective-permute-start.16 = (bf16[1,640,128]{2,1,0:T(8,128)(2,1)S(1)}, bf16[1,640,128]{2,1,0:T(8,128)(2,1)S(1)}, u32[]{:S(2)}, u32[]{:S(2)}) collective-permute-start(bf16[1,640,128]{2,1,0:T(8,128)(2,1)S(1)} %get-tuple-element.35), channel_id=1, source_target_pairs={{0,16},{8,24},{16,0},{24,8},{1,17},{9,25},{17,1},{25,9},{2,18},{10... | collective-permute-start | bytes 491528 | tf_op jit(solution)/shard_map/ppermute | solution.py:309
  140.4 8.5 %collective-permute-start.17 = (bf16[1,640,128]{2,1,0:T(8,128)(2,1)S(1)}, bf16[1,640,128]{2,1,0:T(8,128)(2,1)S(1)}, u32[]{:S(2)}, u32[]{:S(2)}) collective-permute-start(bf16[1,640,128]{2,1,0:T(8,128)(2,1)S(1)} %get-tuple-element.36), channel_id=1, source_target_pairs={{0,24},{8,16},{16,8},{24,0},{1,25},{9,17},{17,9},{25,1},{2,26},{10... | collective-permute-start | bytes 491528 | tf_op jit(solution)/shard_map/ppermute | solution.py:309
